TPU v7x, 512 devices: a whole 4x8x8 slice. The times are simulated.
512 devices in a mesh: grp: 64 (over y, x, core), tp: 8 (over z).
Axes of the slice: x: 4, y: 8, z: 8, core: 2. Of those that a mesh axis runs over, the one named last changes fastest.
Arguments:
- prefill_q: bfloat16 [16384, 4096], P('grp', 'tp'), may hold values from -32 to 32
- prefill_k: bfloat16 [16384, 1024], P('grp', 'tp'), may hold values from -32 to 32
- prefill_v: bfloat16 [16384, 1024], P('grp', 'tp'), may hold values from -6 to 6
- span_offset: int32 [64], P('grp'), may hold values from 0 to 32512
- page_group: int32 [1024, 1], P('grp'), may hold values from 0 to 63; in each aligned block of 16 rows (0 to 15, 16 to 31, ...) at most 2 rows name the same one
- page_request: int32 [1024], P('grp'), may hold values from 0 to 3
- decode_q: bfloat16 [256, 4096], P('grp', 'tp'), may hold values from -24 to 24
- cache_k: bfloat16 [256, 512, 1024], P('grp', None, 'tp'), may hold values from -24 to 24
- cache_v: bfloat16 [256, 512, 1024], P('grp', None, 'tp'), may hold values from -6 to 6
- cache_len: int32 [256], P('grp'), may hold values from 2 to 512, as said below
- out_weight: bfloat16 [4096, 8192], P('tp', 'grp'), may hold values from -0.09375 to 0.09375
Outputs:
- prefill_out: bfloat16 [16384, 4096], P('grp', 'tp')
- decode_out: bfloat16 [256, 8192], P('tp', 'grp')
Inputs may be any that keep to these rules, and one draw needn't show every extreme that they name: `page_group`: among the 16 pages of one span no group is named by more than 2 pages, and some span names one group exactly 2 times. `cache_len`: some request has exactly 512 live slots.
All inputs are finite; a program needn't handle non-finite values.
Results may differ from a plain program's by a relative error of at most 0.014.
Values may be sent and summed in bfloat16 or wider, within the bound.
No kernel may reach another device: no remote copies, remote signals or barrier semaphores. Data moves between devices by JAX's collectives and lax.ppermute only.
A program may use at most 64 MiB of HBM per device.

v0:
```python
import math

import jax
import jax.numpy as jnp
from jax import lax
from jax.sharding import PartitionSpec as P

HD = 128
QPK = 4
PAGE = 16


rope_base = 500000.0
neg_large = -1e30


def rotate(values, positions):
    half_dim = values.shape[-1] // 2
    frequency = rope_base ** (-2.0 * jnp.arange(half_dim, dtype=jnp.float32) / values.shape[-1])
    angle_rad = positions.astype(jnp.float32)[:, None] * frequency[None, :]
    cosine = jnp.cos(angle_rad)[:, None, :]
    sine_part = jnp.sin(angle_rad)[:, None, :]
    lower_half = values[..., :half_dim]
    upper_half = values[..., half_dim:]
    return jnp.concatenate(
        [
            lower_half * cosine - upper_half * sine_part,
            upper_half * cosine + lower_half * sine_part,
        ],
        axis=-1,
    )


def partial_softmax(queries, keys, values, visible):
    score_scale = 1.0 / math.sqrt(HD)
    scores = (
        jnp.einsum("brkgd,bskd->brkgs", queries, keys, preferred_element_type=jnp.float32)
        * score_scale
    )
    key_shown = visible[:, :, None, None, :]
    peak_score = jnp.max(jnp.where(key_shown, scores, neg_large), axis=-1)
    weights = jnp.where(key_shown, jnp.exp(scores - peak_score[..., None]), 0.0)
    total_weight = jnp.sum(weights, axis=-1)
    summed = jnp.einsum("brkgs,bskd->brkgd", weights, values.astype(jnp.float32))
    return (peak_score, total_weight, summed)


def combine(peaks, totals, sums):
    top_peak = jnp.max(peaks, axis=0)
    factor = jnp.exp(peaks - top_peak[None])
    return jnp.sum(factor[..., None] * sums, axis=0) / jnp.sum(factor * totals, axis=0)[..., None]


def on_device(
    prefill_q,
    prefill_k,
    prefill_v,
    span_offset,
    page_group,
    page_request,
    decode_q,
    cache_k,
    cache_v,
    cache_len,
    out_weight,
):
    row_count = prefill_q.shape[0]
    key_heads = prefill_k.shape[1] // HD
    positions = span_offset[0] + jnp.arange(row_count, dtype=jnp.int32)
    query_rot = rotate(
        prefill_q.astype(jnp.float32).reshape(row_count, key_heads * QPK, HD), positions
    ).astype(jnp.bfloat16)
    key_rot = rotate(
        prefill_k.astype(jnp.float32).reshape(row_count, key_heads, HD), positions
    ).astype(jnp.bfloat16)
    value_rows = prefill_v.reshape(row_count, key_heads, HD)
    block_rows = min(row_count, 512)
    block_count = row_count // block_rows
    query_blocks = query_rot.reshape(block_count, block_rows, key_heads, QPK, HD)
    key_place = jnp.arange(row_count, dtype=jnp.int32)

    def attend(block_item):
        query_block, first_row = block_item
        scores = jnp.einsum(
            "qkgd,skd->kgqs", query_block, key_rot, preferred_element_type=jnp.float32
        ) * (1.0 / math.sqrt(HD))
        query_place = first_row + jnp.arange(block_rows, dtype=jnp.int32)
        causal = key_place[None, :] <= query_place[:, None]
        scores = jnp.where(causal, scores, neg_large)
        peak_score = jnp.max(scores, axis=-1, keepdims=True)
        weights = jnp.exp(scores - peak_score)
        weights_low = (weights / jnp.sum(weights, axis=-1, keepdims=True)).astype(jnp.bfloat16)
        return jnp.einsum(
            "kgqs,skd->qkgd", weights_low, value_rows, preferred_element_type=jnp.float32
        ).astype(jnp.bfloat16)

    starts = jnp.arange(block_count, dtype=jnp.int32) * block_rows
    prefill_out = lax.map(attend, (query_blocks, starts)).reshape(row_count, key_heads * QPK * HD)
    groups = lax.axis_size("grp")
    page_count = row_count // PAGE
    capacity = max(2, 2 * page_count // groups)
    target = page_group[:, 0]
    page_index = jnp.arange(page_count, dtype=jnp.int32)
    same_target = target[None, :] == target[:, None]
    earlier = jnp.sum(
        (same_target & (page_index[None, :] < page_index[:, None])).astype(jnp.int32), axis=1
    )
    slot_index = target * capacity + earlier
    placing = jnp.arange(groups * capacity, dtype=jnp.int32)[:, None] == slot_index[None, :]
    onehot = placing.astype(jnp.bfloat16)
    page_width = PAGE * key_heads * HD
    send_k = (
        jnp.dot(onehot, key_rot.reshape(page_count, page_width), preferred_element_type=jnp.float32)
        .astype(jnp.bfloat16)
        .reshape(groups, capacity, page_width)
    )
    send_v = (
        jnp.dot(
            onehot, prefill_v.reshape(page_count, page_width), preferred_element_type=jnp.float32
        )
        .astype(jnp.bfloat16)
        .reshape(groups, capacity, page_width)
    )
    send_req = (
        jnp.sum(placing.astype(jnp.int32) * (page_request + 1)[None, :], axis=1) - 1
    ).reshape(groups, capacity)
    requests = decode_q.shape[0]
    slot_total = cache_k.shape[1]
    queries = decode_q.reshape(requests, key_heads, QPK, HD)
    keys_home = cache_k.reshape(requests, slot_total, key_heads, HD)
    values_home = cache_v.reshape(requests, slot_total, key_heads, HD)
    visible_home = (jnp.arange(slot_total, dtype=jnp.int32)[None, :] < cache_len[:, None])[
        :, None, :
    ]
    resident = partial_softmax(queries[:, None], keys_home, values_home, visible_home)
    resident = tuple((jnp.swapaxes(member, 0, 1) for member in resident))
    request_ids = jnp.arange(requests, dtype=jnp.int32)
    got_k, got_v, got_req = (
        lax.all_to_all(send_k, "grp", split_axis=0, concat_axis=0, tiled=True),
        lax.all_to_all(send_v, "grp", split_axis=0, concat_axis=0, tiled=True),
        lax.all_to_all(send_req, "grp", split_axis=0, concat_axis=0, tiled=True),
    )
    tokens = groups * capacity * PAGE
    new_keys = got_k.reshape(1, tokens, key_heads, HD)
    new_values = got_v.reshape(1, tokens, key_heads, HD)
    owner_req = jnp.repeat(got_req.reshape(-1), PAGE)
    visible = (owner_req[None, :] == request_ids[:, None])[None]
    remote = partial_softmax(queries[None], new_keys, new_values, visible)
    attention = combine(
        jnp.concatenate([resident[0], remote[0]], axis=0),
        jnp.concatenate([resident[1], remote[1]], axis=0),
        jnp.concatenate([resident[2], remote[2]], axis=0),
    )
    attention = attention.reshape(requests, key_heads * QPK * HD).astype(jnp.bfloat16)
    term_rows = jnp.dot(
        lax.all_gather(attention, "grp", axis=0, tiled=True),
        out_weight,
        preferred_element_type=jnp.float32,
    )
    decode_out = lax.psum_scatter(term_rows, "tp", scatter_dimension=0, tiled=True).astype(
        jnp.bfloat16
    )
    return (prefill_out, decode_out)


def solution(mesh):
    in_specs = (
        P("grp", "tp"),
        P("grp", "tp"),
        P("grp", "tp"),
        P("grp"),
        P("grp", None),
        P("grp"),
        P("grp", "tp"),
        P("grp", None, "tp"),
        P("grp", None, "tp"),
        P("grp"),
        P("tp", "grp"),
    )
    out_specs = (P("grp", "tp"), P("tp", "grp"))
    return jax.shard_map(
        on_device, mesh=mesh, in_specs=in_specs, out_specs=out_specs, check_vma=False
    )
```

profile of v0, /device:TPU:2, one launch (start us, length us, event | category | flops | bytes accessed | tf_op | source)
XLA Modules:
  0.0 167.8 jit_solution(10328069334092434891)
XLA Ops:
  7.2 0.7 copy-done.6
  7.9 0.2 convert_reduce_fusion
  8.1 0.5 copy-done.7
  8.6 0.1 select_reduce_fusion.2
  8.7 0.8 sub.71
  9.4 10.7 %all-to-all-start = ((s32[64,1,2]{2,1,0:T(1,128)}), s32[64,1,2]{2,1,0:T(1,128)S(1)}, u32[]{:S(2)}, u32[]{:S(2)}) async-start(s32[64,1,2]{2,1,0:T(1,128)} %bitcast.19), calls=%async_computation | async-start | bytes 65536 | tf_op jit(solution)/shard_map/all_to_all | solution.py:141
  20.1 1.1 copy.29
  21.9 0.1 copy-done.3
  22.0 0.8 copy-done.4
  22.9 0.4 convolution_convert_fusion
  23.3 0.6 fusion.14
  23.9 0.1 pad_maximum_fusion
  24.0 0.4 convolution_convert_fusion.1
  24.4 0.2 copy.40
  24.6 0.2 copy.39
  24.9 1.1 reshape.476
  26.0 1.1 reshape.472
  27.2 1.4 all-to-all-done
  28.6 8.9 %all-to-all-start.1 = ((bf16[64,2,2048]{2,1,0:T(2,128)(2,1)}), bf16[64,2,2048]{2,1,0:T(2,128)(2,1)S(1)}, u32[]{:S(2)}, u32[]{:S(2)}) async-start(bf16[64,2,2048]{2,1,0:T(2,128)(2,1)} %reshape.472), calls=%async_computation.1 | async-start | bytes 1048576 | tf_op jit(solution)/shard_map/all_to_all | solution.py:139
  37.6 0.3 select_reduce_fusion.1
  37.9 0.2 bitcast_reduce_fusion
  38.1 0.4 copy-done.1
  38.5 0.2 convolution_bitcast_fusion.1
  38.8 0.5 multiply_cosine_fusion
  39.3 0.1 subtract_convert_fusion
  39.5 15.6 %all-to-all-done.1 = bf16[64,2,2048]{2,1,0:T(2,128)(2,1)S(1)} async-done(((bf16[64,2,2048]{2,1,0:T(2,128)(2,1)}), bf16[64,2,2048]{2,1,0:T(2,128)(2,1)S(1)}, u32[]{:S(2)}, u32[]{:S(2)}) %all-to-all-start.1) | async-done | bytes 524320 | tf_op jit(solution)/shard_map/all_to_all | solution.py:139
  55.0 5.9 %all-to-all-start.2 = ((bf16[64,2,2048]{2,1,0:T(2,128)(2,1)}), bf16[64,2,2048]{2,1,0:T(2,128)(2,1)S(1)}, u32[]{:S(2)}, u32[]{:S(2)}) async-start(bf16[64,2,2048]{2,1,0:T(2,128)(2,1)} %reshape.476), calls=%async_computation.2 | async-start | bytes 1048576 | tf_op jit(solution)/shard_map/all_to_all | solution.py:140
  61.0 0.4 fusion.41
  61.4 0.5 broadcast.211
  62.0 0.7 reduce.16
  62.7 0.1 reshape.471
  62.9 0.1 eq.51
  63.0 0.3 reshape.488
  63.4 0.4 select_reduce_fusion
  63.7 0.2 fusion.18
  64.0 14.5 %all-to-all-done.2 = bf16[64,2,2048]{2,1,0:T(2,128)(2,1)S(1)} async-done(((bf16[64,2,2048]{2,1,0:T(2,128)(2,1)}), bf16[64,2,2048]{2,1,0:T(2,128)(2,1)S(1)}, u32[]{:S(2)}, u32[]{:S(2)}) %all-to-all-start.2) | async-done | bytes 524320 | tf_op jit(solution)/shard_map/all_to_all | solution.py:140
  78.5 0.3 reshape.489
  78.8 0.3 convolution_bitcast_fusion
  79.1 0.1 fusion.26
  79.2 0.1 divide_convert_fusion.2
  79.3 36.9 %all-gather = bf16[64,4,512]{2,1,0:T(4,128)(2,1)S(1)} all-gather(bf16[1,4,512]{2,1,0:T(4,128)(2,1)S(1)} %reshape.483), channel_id=1, replica_groups=mesh['grp'=64,'tp'=8] {'grp'}, dimensions={0}, use_global_device_ids=true | all-gather | bytes 266240 | tf_op jit(solution)/shard_map/all_gather | solution.py:156
  116.3 0.8 copy-done.2
  117.1 0.9 fusion.42
  118.0 0.2 fusion.4
  118.2 0.3 convolution_convert_fusion.2
  118.5 0.8 copy.35
  119.4 40.3 %reduce-scatter.2.cloned.1.call-done = f32[32,128]{1,0:T(8,128)} async-done(((f32[256,128]{1,0:T(8,128)}), f32[32,128]{1,0:T(8,128)}) %reduce-scatter.2.cloned.1.call-update) | async-done | bytes 16400 | tf_op jit(solution)/shard_map/reduce_scatter | solution.py:160
  159.6 1.3 convert_element_type.72
  (32 shorter events, 0.6 us)
Async XLA Ops:
  7.2 30.4 %copy-start = (bf16[4,512,128]{2,1,0:T(8,128)(2,1)S(1)}, bf16[4,512,128]{2,1,0:T(8,128)(2,1)}, u32[]{:S(2)}) copy-start(bf16[4,512,128]{2,1,0:T(8,128)(2,1)} %param.18) | copy-start | bytes 1572868
  7.2 0.7 copy-start.6
  7.9 0.7 copy-start.7
  9.4 19.2 %all-to-all-start = ((s32[64,1,2]{2,1,0:T(1,128)}), s32[64,1,2]{2,1,0:T(1,128)S(1)}, u32[]{:S(2)}, u32[]{:S(2)}) async-start(s32[64,1,2]{2,1,0:T(1,128)} %bitcast.19), calls=%async_computation | async-start | bytes 65536 | tf_op jit(solution)/shard_map/all_to_all | solution.py:141
  21.2 0.8 copy-start.3
  22.0 0.8 copy-start.4
  26.0 1.2 copy-start.5
  27.2 10.3 %copy-start.8 = (s32[4]{0:T(128)S(1)}, s32[4]{0:T(128)}, u32[]{:S(2)}) copy-start(s32[4]{0:T(128)} %param.20) | copy-start | bytes 52
  28.6 26.5 %all-to-all-start.1 = ((bf16[64,2,2048]{2,1,0:T(2,128)(2,1)}), bf16[64,2,2048]{2,1,0:T(2,128)(2,1)S(1)}, u32[]{:S(2)}, u32[]{:S(2)}) async-start(bf16[64,2,2048]{2,1,0:T(2,128)(2,1)} %reshape.472), calls=%async_computation.1 | async-start | bytes 1048576 | tf_op jit(solution)/shard_map/all_to_all | solution.py:139
  37.5 1.0 copy-start.1
  55.0 23.4 %all-to-all-start.2 = ((bf16[64,2,2048]{2,1,0:T(2,128)(2,1)}), bf16[64,2,2048]{2,1,0:T(2,128)(2,1)S(1)}, u32[]{:S(2)}, u32[]{:S(2)}) async-start(bf16[64,2,2048]{2,1,0:T(2,128)(2,1)} %reshape.476), calls=%async_computation.2 | async-start | bytes 1048576 | tf_op jit(solution)/shard_map/all_to_all | solution.py:140
  60.9 98.7 %reduce-scatter.2.cloned.1.call-start = ((), (), s32[]{:S(2)}) async-start(), calls=%async_computation.4 | async-start | bytes 147456 | tf_op jit(solution)/shard_map/reduce_scatter | solution.py:160
  116.2 0.9 copy-start.2
Sparse Core Ops, SparseCore 0:
  118.1 41.4 reduce-scatter.1
where the time goes:
time: 168 us
  waiting for transfers between devices  71.8 us (43%)
  blocking collectives  36.9 us (22%)
  starting transfers between devices  25.5 us (15%)
  between operations  14.9 us (9%)
  local copies, waits for them, and re-layouts  10.5 us (6%)
  other arithmetic  4.58 us (3%)
  matrix products  3.62 us (2%)
    reduce_scatter x1, waiting for transfers between devices, on_device(): lax.psum_scatter(term_rows, 'tp', scatter_dimension=0, tiled=True)  40.3 us
    all_gather x1, blocking collectives, on_device(): lax.all_gather(attention, 'grp', axis=0, tiled=True)  36.9 us
    all_to_all x1, waiting for transfers between devices, on_device(): lax.all_to_all(send_k, 'grp', split_axis=0, concat_axis=0, tiled=True)  15.6 us
    all_to_all x1, waiting for transfers between devices, on_device(): lax.all_to_all(send_v, 'grp', split_axis=0, concat_axis=0, tiled=True)  14.5 us
    all_to_all x1, starting transfers between devices, on_device(): lax.all_to_all(send_req, 'grp', split_axis=0, concat_axis=0, tiled=True)  10.7 us
    all_to_all x1, starting transfers between devices, on_device(): lax.all_to_all(send_k, 'grp', split_axis=0, concat_axis=0, tiled=True)  8.88 us
    all_to_all x1, starting transfers between devices, on_device(): lax.all_to_all(send_v, 'grp', split_axis=0, concat_axis=0, tiled=True)  5.88 us
    unnamed x24, local copies, waits for them, and re-layouts  5.83 us
  transfers between devices with their start and end apart: 4, of which 4 were waited for; matrix products, arithmetic and copies ran while one was open for 7% of the time, Pallas kernels for 0%

commit v1 on v0

--- a/solution.py
+++ b/solution.py
@@ -135,11 +135,14 @@
     resident = partial_softmax(queries[:, None], keys_home, values_home, visible_home)
     resident = tuple((jnp.swapaxes(member, 0, 1) for member in resident))
     request_ids = jnp.arange(requests, dtype=jnp.int32)
-    got_k, got_v, got_req = (
-        lax.all_to_all(send_k, "grp", split_axis=0, concat_axis=0, tiled=True),
-        lax.all_to_all(send_v, "grp", split_axis=0, concat_axis=0, tiled=True),
-        lax.all_to_all(send_req, "grp", split_axis=0, concat_axis=0, tiled=True),
+    owner_lanes = jnp.broadcast_to(
+        send_req.astype(jnp.bfloat16)[..., None], (groups, capacity, HD)
     )
+    packet = jnp.concatenate([send_k, send_v, owner_lanes], axis=-1)
+    got = lax.all_to_all(packet, "grp", split_axis=0, concat_axis=0, tiled=True)
+    got_k = got[..., :page_width]
+    got_v = got[..., page_width : 2 * page_width]
+    got_req = got[..., 2 * page_width].astype(jnp.int32)
     tokens = groups * capacity * PAGE
     new_keys = got_k.reshape(1, tokens, key_heads, HD)
     new_values = got_v.reshape(1, tokens, key_heads, HD)
@@ -152,14 +155,23 @@
         jnp.concatenate([resident[2], remote[2]], axis=0),
     )
     attention = attention.reshape(requests, key_heads * QPK * HD).astype(jnp.bfloat16)
+    width = attention.shape[1]
+    repeated = jnp.broadcast_to(attention[None], (groups, requests, width))
+    everyone = lax.all_to_all(repeated, "grp", split_axis=0, concat_axis=0, tiled=True)
     term_rows = jnp.dot(
-        lax.all_gather(attention, "grp", axis=0, tiled=True),
+        everyone.reshape(groups * requests, width),
         out_weight,
         preferred_element_type=jnp.float32,
+    ).astype(jnp.bfloat16)
+    shards = lax.axis_size("tp")
+    terms = lax.all_to_all(
+        term_rows.reshape(shards, groups * requests // shards, term_rows.shape[1]),
+        "tp",
+        split_axis=0,
+        concat_axis=0,
+        tiled=True,
     )
-    decode_out = lax.psum_scatter(term_rows, "tp", scatter_dimension=0, tiled=True).astype(
-        jnp.bfloat16
-    )
+    decode_out = jnp.sum(terms.astype(jnp.float32), axis=0).astype(jnp.bfloat16)
     return (prefill_out, decode_out)
 
 

time: 168 us -> 92.5 us (0.55)
  the two profiles are of different devices: /device:TPU:2 before, /device:TPU:1 now
where the time goes in v1:
time: 92.5 us; the launch traced here: 92 us
  waiting for transfers between devices  43.8 us (47%)
  starting transfers between devices  28.3 us (31%)
  other arithmetic  8.37 us (9%)
  local copies, waits for them, and re-layouts  5.22 us (6%)
  matrix products  4.64 us (5%)
  between operations  1.65 us (2%)
    all_to_all x1, waiting for transfers between devices, on_device(): got = lax.all_to_all(packet, 'grp', split_axis=0, concat_axis=0, tiled=True)  25.2 us
    all_to_all x1, waiting for transfers between devices, on_device(): lax.all_to_all(repeated, 'grp', split_axis=0, concat_axis=0, tiled=True)  12.5 us
    all_to_all x1, starting transfers between devices, on_device(): got = lax.all_to_all(packet, 'grp', split_axis=0, concat_axis=0, tiled=True)  11.8 us
    all_to_all x1, starting transfers between devices, on_device(): lax.all_to_all(term_rows.reshape(shards, groups * requests // shards, ter...  10 us
    all_to_all x1, starting transfers between devices, on_device(): lax.all_to_all(repeated, 'grp', split_axis=0, concat_axis=0, tiled=True)  6.51 us
    all_to_all x1, waiting for transfers between devices, on_device(): lax.all_to_all(term_rows.reshape(shards, groups * requests // shards, ter...  6.05 us
  transfers between devices with their start and end apart: 3, of which 3 were waited for; matrix products, arithmetic and copies ran while one was open for 5% of the time, Pallas kernels for 0%

profile of v1, /device:TPU:1, one launch (start us, length us, event | category | flops | bytes accessed | tf_op | source)
XLA Modules:
  0.0 92.0 jit_solution(16989337654159191366)
XLA Ops:
  1.4 0.9 bitcast_convert_fusion
  2.2 0.6 fusion.14
  2.8 0.1 pad_maximum_fusion.1
  3.0 0.9 convert_reduce_fusion.1
  3.9 0.7 multiply_add_fusion
  4.6 0.4 convolution_convert_fusion.1
  5.0 0.3 reshape.482
  5.3 0.1 select_reduce_fusion.2
  5.4 0.1 convert_element_type.94
  5.6 0.4 convolution_convert_fusion
  6.0 0.3 reshape.484
  6.4 0.1 broadcast_in_dim.98
  6.5 1.8 %pad_maximum_fusion = bf16[64,2,4224]{2,1,0:T(2,128)(2,1)} fusion(bf16[64,2,128]{2,1,0:T(2,128)(2,1)S(1)} %broadcast_in_dim.98, bf16[64,2,2048]{2,1,0:T(2,128)(2,1)S(1)} %reshape.484, bf16[64,2,2048]{2,1,0:T(2,128)(2,1)S(1)} %reshape.482), kind=kLoop, calls=%fused_computation.13 | loop fusion | flops 3244032 | bytes 2162688 | tf_op jit(solution)/shard_map/concatenate | solution.py:141
  8.3 11.8 %all-to-all-start = ((bf16[64,2,4224]{2,1,0:T(2,128)(2,1)}), bf16[64,2,4224]{2,1,0:T(2,128)(2,1)S(1)}, u32[]{:S(2)}, u32[]{:S(2)}) async-start(bf16[64,2,4224]{2,1,0:T(2,128)(2,1)} %pad_maximum_fusion), calls=%async_computation | async-start | bytes 2162688 | tf_op jit(solution)/shard_map/all_to_all | solution.py:142
  20.1 0.1 copy.40
  20.3 0.2 copy.49
  20.5 0.2 copy.50
  20.7 0.2 copy-done.5
  20.9 0.1 iota_compare_fusion.6
  21.0 0.3 select_reduce_fusion.1
  21.3 0.2 bitcast_reduce_fusion
  21.5 1.3 %convolution_bitcast_fusion.1 = f32[1,4,1,4,128]{4,3,1,0,2:T(4,128)S(1)} fusion(bf16[4,512,128]{2,1,0:T(8,128)(2,1)} %param.19, f32[4,1,512,1,4]{2,4,0,3,1:T(4,128)S(1)} %get-tuple-element.43, f32[4,4]{1,0:T(4,128)S(1)} %get-tuple-element.42, pred[4,512]{1,0:T(4,128)(4,1)S(1)} %iota_compare_fusion.6), kind=kOutput, calls=%fused_computation.12 | convolution fusion | flops 2113536 | bytes 567360 | tf_op jit(solution)/shard_map/brkgs,bskd->brkgd/dot_general | solution.py:44
  22.8 0.5 multiply_cosine_fusion
  23.4 0.1 subtract_convert_fusion
  23.5 25.2 %all-to-all-done = bf16[64,2,4224]{2,1,0:T(2,128)(2,1)S(1)} async-done(((bf16[64,2,4224]{2,1,0:T(2,128)(2,1)}), bf16[64,2,4224]{2,1,0:T(2,128)(2,1)S(1)}, u32[]{:S(2)}, u32[]{:S(2)}) %all-to-all-start) | async-done | bytes 1081376 | tf_op jit(solution)/shard_map/all_to_all | solution.py:142
  48.7 1.2 %convert_reduce_fusion = s32[64,2]{1,0:T(8,128)S(1)} fusion(bf16[64,2,4224]{2,1,0:T(2,128)(2,1)S(1)} %all-to-all-done), kind=kLoop, calls=%fused_computation.46 | loop fusion | flops 128 | bytes 768 | tf_op jit(solution)/shard_map/convert_element_type | solution.py:145
  49.9 0.1 reshape.495
  50.0 0.1 broadcast_in_dim.99
  50.1 0.1 eq.51
  50.2 0.7 fusion.41
  50.9 0.3 reshape.498
  51.3 0.4 select_reduce_fusion
  51.7 0.2 fusion.18
  51.9 0.3 reshape.499
  52.2 0.3 convolution_bitcast_fusion
  52.5 0.1 fusion.26
  52.6 0.1 fusion.37
  52.7 0.8 broadcast_in_dim.104
  53.5 6.5 %all-to-all-start.1 = ((bf16[64,4,512]{2,1,0:T(4,128)(2,1)}), bf16[64,4,512]{2,1,0:T(4,128)(2,1)S(1)}, u32[]{:S(2)}, u32[]{:S(2)}) async-start(bf16[64,4,512]{2,1,0:T(4,128)(2,1)} %broadcast_in_dim.104), calls=%async_computation.1 | async-start | bytes 524288 | tf_op jit(solution)/shard_map/all_to_all | solution.py:160
  60.0 0.4 fusion.43
  60.5 0.2 fusion.4
  60.6 12.5 %all-to-all-done.1 = bf16[64,4,512]{2,1,0:T(4,128)(2,1)S(1)} async-done(((bf16[64,4,512]{2,1,0:T(4,128)(2,1)}), bf16[64,4,512]{2,1,0:T(4,128)(2,1)S(1)}, u32[]{:S(2)}, u32[]{:S(2)}) %all-to-all-start.1) | async-done | bytes 262176 | tf_op jit(solution)/shard_map/all_to_all | solution.py:160
  73.2 0.8 convolution_convert_fusion.3
  74.1 10.0 %all-to-all-start.2 = ((bf16[8,32,128]{2,1,0:T(8,128)(2,1)}), bf16[8,32,128]{2,1,0:T(8,128)(2,1)S(1)}, u32[]{:S(2)}, u32[]{:S(2)}) async-start(bf16[8,32,128]{2,1,0:T(8,128)(2,1)} %bitcast.35), calls=%async_computation.2 | async-start | bytes 131072 | tf_op jit(solution)/shard_map/all_to_all | solution.py:167
  84.1 0.3 convolution_convert_fusion.2
  84.5 0.8 copy.45
  85.3 6.0 %all-to-all-done.2 = bf16[8,32,128]{2,1,0:T(8,128)(2,1)S(1)} async-done(((bf16[8,32,128]{2,1,0:T(8,128)(2,1)}), bf16[8,32,128]{2,1,0:T(8,128)(2,1)S(1)}, u32[]{:S(2)}, u32[]{:S(2)}) %all-to-all-start.2) | async-done | bytes 65568 | tf_op jit(solution)/shard_map/all_to_all | solution.py:167
  91.4 0.6 reduce_sum.83
  (25 shorter events, 0.3 us)
Async XLA Ops:
  0.6 20.4 %copy-start = (bf16[4,512,128]{2,1,0:T(8,128)(2,1)S(1)}, bf16[4,512,128]{2,1,0:T(8,128)(2,1)}, u32[]{:S(2)}) copy-start(bf16[4,512,128]{2,1,0:T(8,128)(2,1)} %param.18) | copy-start | bytes 1572868
  2.8 2.8 %copy-start.3 = (bf16[256,128]{1,0:T(8,128)(2,1)S(1)}, bf16[256,128]{1,0:T(8,128)(2,1)}, u32[]{:S(2)}) copy-start(bf16[256,128]{1,0:T(8,128)(2,1)} %param.13) | copy-start | bytes 196612
  8.3 11.8 %copy-start.4 = (bf16[4,512]{1,0:T(4,128)(2,1)S(1)}, bf16[4,512]{1,0:T(4,128)(2,1)}, u32[]{:S(2)}) copy-start(bf16[4,512]{1,0:T(4,128)(2,1)} %param.17) | copy-start | bytes 12292
  8.3 11.8 %copy-start.1 = (bf16[256,512]{1,0:T(8,128)(2,1)S(1)}, bf16[256,512]{1,0:T(8,128)(2,1)}, u32[]{:S(2)}) copy-start(bf16[256,512]{1,0:T(8,128)(2,1)} %param.11) | copy-start | bytes 786436
  8.3 40.4 %all-to-all-start = ((bf16[64,2,4224]{2,1,0:T(2,128)(2,1)}), bf16[64,2,4224]{2,1,0:T(2,128)(2,1)S(1)}, u32[]{:S(2)}, u32[]{:S(2)}) async-start(bf16[64,2,4224]{2,1,0:T(2,128)(2,1)} %pad_maximum_fusion), calls=%async_computation | async-start | bytes 2162688 | tf_op jit(solution)/shard_map/all_to_all | solution.py:142
  20.3 0.7 copy-start.5
  53.5 19.7 %all-to-all-start.1 = ((bf16[64,4,512]{2,1,0:T(4,128)(2,1)}), bf16[64,4,512]{2,1,0:T(4,128)(2,1)S(1)}, u32[]{:S(2)}, u32[]{:S(2)}) async-start(bf16[64,4,512]{2,1,0:T(4,128)(2,1)} %broadcast_in_dim.104), calls=%async_computation.1 | async-start | bytes 524288 | tf_op jit(solution)/shard_map/all_to_all | solution.py:160
  60.5 12.8 %copy-start.2 = (bf16[512,128]{1,0:T(8,128)(2,1)S(1)}, bf16[512,128]{1,0:T(8,128)(2,1)}, u32[]{:S(2)}) copy-start(bf16[512,128]{1,0:T(8,128)(2,1)} %param.21) | copy-start | bytes 393220
  74.1 17.3 %all-to-all-start.2 = ((bf16[8,32,128]{2,1,0:T(8,128)(2,1)}), bf16[8,32,128]{2,1,0:T(8,128)(2,1)S(1)}, u32[]{:S(2)}, u32[]{:S(2)}) async-start(bf16[8,32,128]{2,1,0:T(8,128)(2,1)} %bitcast.35), calls=%async_computation.2 | async-start | bytes 131072 | tf_op jit(solution)/shard_map/all_to_all | solution.py:167

commit v2 on v0

v2 whole, which is shorter than its diff:
```python
import math

import jax
import jax.numpy as jnp
from jax import lax
from jax.experimental import pallas as pl
from jax.experimental.pallas import tpu as pltpu
from jax.sharding import Mesh, PartitionSpec as P

HD = 128
QPK = 4
PAGE = 16
CAP = 2
REQ = 4
ROWS = QPK * REQ

rope_base = 500000.0
neg_large = -1e30
scale = 1.0 / math.sqrt(HD)
f32 = jnp.float32
bf16 = jnp.bfloat16
vmem_limit = 32 * 1024 * 1024


def rotate(values, positions):
    half_dim = values.shape[-1] // 2
    frequency = rope_base ** (-2.0 * jnp.arange(half_dim, dtype=f32) / values.shape[-1])
    angle_rad = positions.astype(f32)[:, None] * frequency[None, :]
    cosine = jnp.cos(angle_rad)[:, None, :]
    sine_part = jnp.sin(angle_rad)[:, None, :]
    lower_half = values[..., :half_dim]
    upper_half = values[..., half_dim:]
    return jnp.concatenate(
        [
            lower_half * cosine - upper_half * sine_part,
            upper_half * cosine + lower_half * sine_part,
        ],
        axis=-1,
    )


def dot(a, b, dims):
    return lax.dot_general(a, b, (dims, ((), ())), preferred_element_type=f32)


def iota(shape, axis):
    return lax.broadcasted_iota(jnp.int32, shape, axis)


def call(kernel, outs, *args):
    return pl.pallas_call(
        kernel,
        out_shape=outs,
        compiler_params=pltpu.CompilerParams(vmem_limit_bytes=vmem_limit),
    )(*args)


def resident_kernel(q_ref, k_ref, v_ref, len_ref, sum_ref, peak_ref, total_ref):
    q = q_ref[...].astype(f32)
    rows = jnp.concatenate([q[:, h * HD : (h + 1) * HD] for h in range(QPK)], axis=0).astype(bf16)
    slots = k_ref.shape[1]
    request = iota((ROWS, 1), 0) % REQ
    live = jnp.zeros((ROWS, 1), jnp.int32)
    scores = jnp.zeros((ROWS, slots), f32)
    for r in range(REQ):
        live = jnp.where(request == r, len_ref[:, r : r + 1], live)
        scores = jnp.where(request == r, dot(rows, k_ref[r], ((1,), (1,))), scores)
    shown = iota((ROWS, slots), 1) < live
    scores = jnp.where(shown, scores * scale, neg_large)
    peak = jnp.max(scores, axis=1, keepdims=True)
    weights = jnp.where(shown, jnp.exp(scores - peak), 0.0)
    total = jnp.sum(weights, axis=1, keepdims=True)
    low = weights.astype(bf16)
    summed = jnp.zeros((ROWS, HD), f32)
    for r in range(REQ):
        summed = jnp.where(request == r, dot(low, v_ref[r], ((1,), (0,))), summed)
    sum_ref[...] = summed
    peak_ref[...] = jnp.broadcast_to(peak, (ROWS, HD))
    total_ref[...] = jnp.broadcast_to(total, (ROWS, HD))


def parts_of(value, count):
    parts = []
    for _ in range(count):
        part = value.astype(bf16).astype(f32)
        parts.append(part)
        value = value - part
    return parts


def page_kernel(q_ref, k_ref, v_ref, owner_ref, slot_ref, place_ref, out_ref):
    pages = owner_ref.shape[0]
    tokens = k_ref.shape[0]
    chosen = (iota((pages, q_ref.shape[0]), 1) == owner_ref[...]).astype(f32).astype(bf16)
    queries = dot(chosen, q_ref[...], ((1,), (0,))).astype(bf16)
    own = (iota((pages, tokens), 1) // PAGE) == iota((pages, tokens), 0)
    lane = iota((pages, HD), 1)
    extra = jnp.where(lane // ROWS == 5, place_ref[...].astype(f32), 0.0)
    columns = []
    for h in range(QPK):
        scores = dot(queries[:, h * HD : (h + 1) * HD], k_ref[...], ((1,), (1,))) * scale
        scores = jnp.where(own, scores, neg_large)
        peak = jnp.max(scores, axis=1, keepdims=True)
        weights = jnp.where(own, jnp.exp(scores - peak), 0.0)
        total = jnp.sum(weights, axis=1, keepdims=True)
        columns.append(dot(weights.astype(bf16), v_ref[...], ((1,), (0,))) / total)
        for block, part in enumerate(parts_of(peak, 3) + parts_of(total, 2)):
            extra = jnp.where(lane // REQ == block * QPK + h, part, extra)
    payload = jnp.concatenate(columns + [extra], axis=1).astype(bf16)
    placing = (iota((pages, out_ref.shape[0]), 1) == slot_ref[...]).astype(f32).astype(bf16)
    out_ref[...] = dot(placing, payload, ((0,), (0,))).astype(bf16)


def combine_kernel(got_ref, sum_ref, peak_ref, total_ref, out_ref):
    slots = got_ref.shape[0]
    extra = got_ref[:, QPK * HD :].astype(f32)
    block = [extra] + [pltpu.roll(extra, HD - ROWS * i, 1) for i in range(1, 6)]
    lane = iota((slots, HD), 1)
    shown = (block[5] == (lane % REQ + 1).astype(f32)) & (lane < ROWS)
    peaks = jnp.where(shown, block[0] + block[1] + block[2], neg_large)
    totals = block[3] + block[4]
    eye = iota((ROWS, HD), 0) == iota((ROWS, HD), 1)
    home_peak = jnp.sum(jnp.where(eye, peak_ref[...], 0.0), axis=0, keepdims=True)
    home_total = jnp.sum(jnp.where(eye, total_ref[...], 0.0), axis=0, keepdims=True)
    top = jnp.maximum(jnp.max(peaks, axis=0, keepdims=True), home_peak)
    weights = jnp.where(shown, jnp.exp(peaks - top) * totals, 0.0)
    home = jnp.exp(home_peak - top)
    whole = jnp.sum(weights, axis=0, keepdims=True) + home * home_total
    whole = jnp.where(iota((1, HD), 1) < ROWS, whole, 1.0)
    low = (weights / whole).astype(bf16)[:, :ROWS]
    home_column = jnp.sum(jnp.where(eye, home / whole, 0.0), axis=1, keepdims=True)
    rows = sum_ref[...] * home_column
    head = iota((ROWS, HD), 0) // REQ
    for h in range(QPK):
        add = dot(low, got_ref[:, h * HD : (h + 1) * HD], ((0,), (0,)))
        rows = rows + jnp.where(head == h, add, 0.0)
    wide = jnp.concatenate([rows[h * REQ : (h + 1) * REQ, :] for h in range(QPK)], axis=1)
    out_ref[...] = jnp.broadcast_to(wide[None], out_ref.shape).astype(bf16)


def on_device(
    prefill_q,
    prefill_k,
    prefill_v,
    span_offset,
    page_group,
    page_request,
    decode_q,
    cache_k,
    cache_v,
    cache_len,
    out_weight,
):
    grp = ("y", "x", "c")
    groups = lax.axis_size(grp)
    row_count = prefill_q.shape[0]
    width = decode_q.shape[1]

    asked = lax.all_to_all(
        jnp.broadcast_to(decode_q[None], (groups,) + decode_q.shape),
        grp,
        split_axis=0,
        concat_axis=0,
        tiled=True,
    ).reshape(groups * REQ, width)

    steps = lax.axis_size("x")
    here = lax.axis_index("x")
    pieces = [out_weight] + [
        lax.ppermute(out_weight, "x", [((i + k) % steps, i) for i in range(steps)])
        for k in range(1, steps)
    ]
    columns = jnp.roll(jnp.stack(pieces), here, axis=0)

    positions = span_offset[0] + jnp.arange(row_count, dtype=jnp.int32)
    key_rot = rotate(prefill_k.astype(f32).reshape(row_count, 1, HD), positions).astype(bf16)
    query_rot = rotate(prefill_q.astype(f32).reshape(row_count, QPK, HD), positions).astype(bf16)
    scores = jnp.einsum("qgd,sd->gqs", query_rot, key_rot[:, 0], preferred_element_type=f32) * scale
    place = jnp.arange(row_count, dtype=jnp.int32)
    scores = jnp.where(place[None, :] <= place[:, None], scores, neg_large)
    weights = jnp.exp(scores - jnp.max(scores, axis=-1, keepdims=True))
    weights_low = (weights / jnp.sum(weights, axis=-1, keepdims=True)).astype(bf16)
    prefill_out = (
        jnp.einsum("gqs,sd->qgd", weights_low, prefill_v, preferred_element_type=f32)
        .astype(bf16)
        .reshape(row_count, QPK * HD)
    )

    target = page_group[:, 0]
    page_index = jnp.arange(target.shape[0], dtype=jnp.int32)
    same_target = target[None, :] == target[:, None]
    earlier = jnp.sum(
        (same_target & (page_index[None, :] < page_index[:, None])).astype(jnp.int32), axis=1
    )
    slot_index = (target * CAP + earlier)[:, None]
    owner = (target * REQ + page_request)[:, None]

    rows_of = jax.ShapeDtypeStruct((ROWS, HD), f32)
    home = call(
        resident_kernel, (rows_of,) * 3, decode_q, cache_k, cache_v, cache_len.reshape(1, REQ)
    )
    sent = call(
        page_kernel,
        jax.ShapeDtypeStruct((groups * CAP, width + HD), bf16),
        asked,
        key_rot[:, 0],
        prefill_v,
        owner,
        slot_index,
        (page_request + 1)[:, None],
    )
    got = lax.all_to_all(
        sent.reshape(groups, CAP, width + HD), grp, split_axis=0, concat_axis=0, tiled=True
    ).reshape(groups * CAP, width + HD)

    peers = lax.axis_size(("y", "c"))
    repeated = call(
        combine_kernel, jax.ShapeDtypeStruct((peers, REQ, width), bf16), got, *home
    )
    everyone = lax.all_to_all(repeated, ("y", "c"), split_axis=0, concat_axis=0, tiled=True)
    everyone = everyone.reshape(peers * REQ, width)
    shards = lax.axis_size("z")
    terms = jnp.einsum("ad,xdc->xac", everyone, columns, preferred_element_type=f32).astype(bf16)
    terms = terms.reshape(steps * shards, peers * REQ // shards, HD)
    terms = lax.all_to_all(terms, ("x", "z"), split_axis=0, concat_axis=0, tiled=True)
    terms = terms.reshape(steps, shards, peers * REQ // shards, HD)
    decode_out = jnp.sum(terms.astype(f32), axis=1).astype(bf16).reshape(-1, HD)
    return (prefill_out, decode_out)


def solution(mesh):
    fine = Mesh(mesh.devices.reshape(8, 4, 2, 8), ("y", "x", "c", "z"))
    grp = ("y", "x", "c")
    in_specs = (
        P(grp, "z"),
        P(grp, "z"),
        P(grp, "z"),
        P(grp),
        P(grp, None),
        P(grp),
        P(grp, "z"),
        P(grp, None, "z"),
        P(grp, None, "z"),
        P(grp),
        P("z", grp),
    )
    out_specs = (P(grp, "z"), P("z", grp))
    return jax.shard_map(
        on_device, mesh=fine, in_specs=in_specs, out_specs=out_specs, check_vma=False
    )
```

time: 168 us -> 93.8 us (0.56)
  the two profiles are of different devices: /device:TPU:2 before, /device:TPU:1 now
where the time goes in v2:
time: 93.8 us; the launch traced here: 93.2 us
  starting transfers between devices  44.8 us (48%)
  waiting for transfers between devices  27.6 us (29%)
  local copies, waits for them, and re-layouts  11.9 us (13%)
  Pallas kernels  2.87 us (3%)
  matrix products  2.21 us (2%)
  other arithmetic  2.2 us (2%)
  between operations  1.57 us (2%)
    all_to_all x1, starting transfers between devices, on_device(): lax.all_to_all(terms, ('x', 'z'), split_axis=0, concat_axis=0, tiled=True)  11.2 us
    all_to_all x1, starting transfers between devices, on_device(): lax.all_to_all(jnp.broadcast_to(decode_q[None], (groups,) + decode_q.shap...  11.1 us
    ppermute x3, starting transfers between devices, on_device(): lax.ppermute(out_weight, 'x', [((i + k) % steps, i) for i in range(steps)])  10.2 us
    all_to_all x1, waiting for transfers between devices, on_device(): lax.all_to_all(sent.reshape(groups, CAP, width + HD), grp, split_axis=0,...  9.83 us
    unnamed x33, local copies, waits for them, and re-layouts  9.28 us
    all_to_all x1, starting transfers between devices, on_device(): lax.all_to_all(sent.reshape(groups, CAP, width + HD), grp, split_axis=0,...  8.69 us
    all_to_all x1, waiting for transfers between devices, on_device(): lax.all_to_all(repeated, ('y', 'c'), split_axis=0, concat_axis=0, tiled=T...  7.82 us
    all_to_all x1, waiting for transfers between devices, on_device(): lax.all_to_all(terms, ('x', 'z'), split_axis=0, concat_axis=0, tiled=True)  7.6 us
  transfers between devices with their start and end apart: 7, of which 4 were waited for; matrix products, arithmetic and copies ran while one was open for 14% of the time, Pallas kernels for 1%

profile of v2, /device:TPU:1, one launch (start us, length us, event | category | flops | bytes accessed | tf_op | source)
XLA Modules:
  0.0 93.2 jit_solution(7573624347139090613)
XLA Ops:
  0.6 5.2 %collective-permute-start = (bf16[512,128]{1,0:T(8,128)(2,1)}, bf16[512,128]{1,0:T(8,128)(2,1)}, u32[]{:S(2)}, u32[]{:S(2)}) collective-permute-start(bf16[512,128]{1,0:T(8,128)(2,1)} %param.21), channel_id=1, source_target_pairs={{16,0},{32,16},{48,32},{0,48},{17,1},{33,17},{49,33},{1,49},{18,2}... | collective-permute-start | bytes 393224 | tf_op jit(solution)/shard_map/ppermute | solution.py:170
  5.9 2.4 %collective-permute-start.1 = (bf16[512,128]{1,0:T(8,128)(2,1)}, bf16[512,128]{1,0:T(8,128)(2,1)}, u32[]{:S(2)}, u32[]{:S(2)}) collective-permute-start(bf16[512,128]{1,0:T(8,128)(2,1)} %param.21), channel_id=1, source_target_pairs={{32,0},{48,16},{0,32},{16,48},{33,1},{49,17},{1,33},{17,49},{34,2}... | collective-permute-start | bytes 393224 | tf_op jit(solution)/shard_map/ppermute | solution.py:170
  8.3 2.5 %collective-permute-start.2 = (bf16[512,128]{1,0:T(8,128)(2,1)}, bf16[512,128]{1,0:T(8,128)(2,1)S(1)}, u32[]{:S(2)}, u32[]{:S(2)}) collective-permute-start(bf16[512,128]{1,0:T(8,128)(2,1)} %param.21), channel_id=1, source_target_pairs={{48,0},{0,16},{16,32},{32,48},{49,1},{1,17},{17,33},{33,49},{50,2}... | collective-permute-start | bytes 393224 | tf_op jit(solution)/shard_map/ppermute | solution.py:170
  10.8 1.5 %broadcast_in_dim.14 = bf16[64,4,512]{2,1,0:T(4,128)(2,1)} broadcast(bf16[4,512]{1,0:T(4,128)(2,1)} %q_ref.1), dimensions={1,2} | broadcast | bytes 266240 | tf_op jit(solution)/shard_map/broadcast_in_dim | solution.py:160
  12.3 11.1 %all-to-all-start = ((bf16[64,4,512]{2,1,0:T(4,128)(2,1)}), bf16[64,4,512]{2,1,0:T(4,128)(2,1)S(1)}, u32[]{:S(2)}, u32[]{:S(2)}) async-start(bf16[64,4,512]{2,1,0:T(4,128)(2,1)} %broadcast_in_dim.14), calls=%async_computation | async-start | bytes 524288 | tf_op jit(solution)/shard_map/all_to_all | solution.py:159
  23.4 0.7 bitcast_dynamic-update-slice_fusion.6
  24.8 0.1 copy-done.8
  24.9 0.5 multiply_cosine_fusion
  25.5 0.0 copy-start.9
  25.5 0.6 fusion.24
  26.1 0.0 copy-done.9
  26.1 0.0 copy-done.10
  26.1 0.1 copy.44.owner_ref
  26.2 0.1 copy.46.place_ref
  26.3 0.2 convert_reduce_fusion
  26.5 0.1 copy.45.slot_ref
  26.6 0.1 copy.40
  26.8 0.2 copy.49
  27.0 0.2 copy.50
  27.2 0.1 pad_maximum_fusion.k_ref
  27.3 0.5 copy-done.1
  27.8 0.3 copy-done
  28.1 0.5 shard_map.123
  28.6 0.1 subtract_convert_fusion
  28.8 0.4 fusion.4
  29.2 0.6 fusion.34
  29.7 1.6 %bitcast_dynamic-update-slice_fusion.4 = bf16[8,512,128]{2,1,0:T(8,128)(2,1)} fusion(bf16[8,512,128]{2,1,0:T(8,128)(2,1)} %bitcast_dynamic-update-slice_fusion.6, bf16[512,128]{1,0:T(8,128)(2,1)} %collective-permute-done), kind=kLoop, calls=%fused_computation.32 | loop fusion | bytes 262144
  31.3 1.6 %bitcast_dynamic-update-slice_fusion.2 = bf16[8,512,128]{2,1,0:T(8,128)(2,1)} fusion(bf16[8,512,128]{2,1,0:T(8,128)(2,1)} %bitcast_dynamic-update-slice_fusion.4, bf16[512,128]{1,0:T(8,128)(2,1)} %collective-permute-done.1), kind=kLoop, calls=%fused_computation.30 | loop fusion | bytes 262144
  32.9 0.7 bitcast_dynamic-update-slice_fusion
  33.5 0.7 bitcast_dynamic-update-slice_fusion.7
  34.2 2.4 %all-to-all-done = bf16[64,4,512]{2,1,0:T(4,128)(2,1)S(1)} async-done(((bf16[64,4,512]{2,1,0:T(4,128)(2,1)}), bf16[64,4,512]{2,1,0:T(4,128)(2,1)S(1)}, u32[]{:S(2)}, u32[]{:S(2)}) %all-to-all-start) | async-done | bytes 262176 | tf_op jit(solution)/shard_map/all_to_all | solution.py:159
  36.5 0.1 reshape.169.q_ref
  36.6 1.4 %shard_map.122 = bf16[128,640]{1,0:T(8,128)(2,1)S(1)} custom-call(bf16[256,512]{1,0:T(8,128)(2,1)S(1)} %reshape.169.q_ref, bf16[256,128]{1,0:T(8,128)(2,1)S(1)} %pad_maximum_fusion.k_ref, bf16[256,128]{1,0:T(8,128)(2,1)S(1)} %copy-done.2, s32[16,1]{1,0:T(8,128)S(1)} %copy.44.owner_ref, s32[16,1]{1,0:T(8,128)S(1)} %copy.45.slot_ref, s32[16,1]{1,0:T(8,128)S(1)} %copy.46.place_ref), custom_call_target="tpu_custom_call" | custom-call | tf_op jit(solution)/shard_map/pallas_call | solution.py:51
  38.0 0.7 reshape.170
  38.7 8.7 %all-to-all-start.1 = ((bf16[64,2,640]{2,1,0:T(2,128)(2,1)}), bf16[64,2,640]{2,1,0:T(2,128)(2,1)S(1)}, u32[]{:S(2)}, u32[]{:S(2)}) async-start(bf16[64,2,640]{2,1,0:T(2,128)(2,1)} %reshape.170), calls=%async_computation.1 | async-start | bytes 327680 | tf_op jit(solution)/shard_map/all_to_all | solution.py:212
  47.4 0.9 bitcast_dynamic-update-slice_fusion.5
  48.4 0.9 bitcast_dynamic-update-slice_fusion.3
  49.3 9.8 %all-to-all-done.1 = bf16[64,2,640]{2,1,0:T(2,128)(2,1)S(1)} async-done(((bf16[64,2,640]{2,1,0:T(2,128)(2,1)}), bf16[64,2,640]{2,1,0:T(2,128)(2,1)S(1)}, u32[]{:S(2)}, u32[]{:S(2)}) %all-to-all-start.1) | async-done | bytes 163872 | tf_op jit(solution)/shard_map/all_to_all | solution.py:212
  59.1 0.1 reshape.171.got_ref
  59.2 1.0 %shard_map.124 = bf16[16,4,512]{2,1,0:T(4,128)(2,1)} custom-call(bf16[128,640]{1,0:T(8,128)(2,1)S(1)} %reshape.171.got_ref, f32[16,128]{1,0:T(8,128)S(1)} %get-tuple-element.5.sum_ref, f32[16,128]{1,0:T(8,128)S(1)} %get-tuple-element.6.peak_ref, f32[16,128]{1,0:T(8,128)S(1)} %get-tuple-element.7.total_ref), custom_call_target="tpu_custom_call" | custom-call | tf_op jit(solution)/shard_map/pallas_call | solution.py:51
  60.2 3.7 %all-to-all-start.2 = ((bf16[16,4,512]{2,1,0:T(4,128)(2,1)}), bf16[16,4,512]{2,1,0:T(4,128)(2,1)S(1)}, u32[]{:S(2)}, u32[]{:S(2)}) async-start(bf16[16,4,512]{2,1,0:T(4,128)(2,1)} %shard_map.124), calls=%async_computation.2 | async-start | bytes 131072 | tf_op jit(solution)/shard_map/all_to_all | solution.py:220
  63.9 7.8 %all-to-all-done.2 = bf16[16,4,512]{2,1,0:T(4,128)(2,1)S(1)} async-done(((bf16[16,4,512]{2,1,0:T(4,128)(2,1)}), bf16[16,4,512]{2,1,0:T(4,128)(2,1)S(1)}, u32[]{:S(2)}, u32[]{:S(2)}) %all-to-all-start.2) | async-done | bytes 65568 | tf_op jit(solution)/shard_map/all_to_all | solution.py:220
  71.7 0.8 convolution_convert_fusion.1
  72.6 11.2 %all-to-all-start.3 = ((bf16[32,8,128]{2,1,0:T(8,128)(2,1)}), bf16[32,8,128]{2,1,0:T(8,128)(2,1)S(1)}, u32[]{:S(2)}, u32[]{:S(2)}) async-start(bf16[32,8,128]{2,1,0:T(8,128)(2,1)} %bitcast.22), calls=%async_computation.3 | async-start | bytes 131072 | tf_op jit(solution)/shard_map/all_to_all | solution.py:225
  83.7 0.4 convolution_convert_fusion
  84.2 0.8 copy.47
  85.0 7.6 %all-to-all-done.3 = bf16[32,8,128]{2,1,0:T(8,128)(2,1)S(1)} async-done(((bf16[32,8,128]{2,1,0:T(8,128)(2,1)}), bf16[32,8,128]{2,1,0:T(8,128)(2,1)S(1)}, u32[]{:S(2)}, u32[]{:S(2)}) %all-to-all-start.3) | async-done | bytes 65568 | tf_op jit(solution)/shard_map/all_to_all | solution.py:225
  92.6 0.6 bitcast_reduce_fusion
  (28 shorter events, 0.2 us)
Async XLA Ops:
  0.6 29.1 %collective-permute-start = (bf16[512,128]{1,0:T(8,128)(2,1)}, bf16[512,128]{1,0:T(8,128)(2,1)}, u32[]{:S(2)}, u32[]{:S(2)}) collective-permute-start(bf16[512,128]{1,0:T(8,128)(2,1)} %param.21), channel_id=1, source_target_pairs={{16,0},{32,16},{48,32},{0,48},{17,1},{33,17},{49,33},{1,49},{18,2}... | collective-permute-start | bytes 393224 | tf_op jit(solution)/shard_map/ppermute | solution.py:170
  5.9 25.5 %collective-permute-start.1 = (bf16[512,128]{1,0:T(8,128)(2,1)}, bf16[512,128]{1,0:T(8,128)(2,1)}, u32[]{:S(2)}, u32[]{:S(2)}) collective-permute-start(bf16[512,128]{1,0:T(8,128)(2,1)} %param.21), channel_id=1, source_target_pairs={{32,0},{48,16},{0,32},{16,48},{33,1},{49,17},{1,33},{17,49},{34,2}... | collective-permute-start | bytes 393224 | tf_op jit(solution)/shard_map/ppermute | solution.py:170
  8.3 24.6 %collective-permute-start.2 = (bf16[512,128]{1,0:T(8,128)(2,1)}, bf16[512,128]{1,0:T(8,128)(2,1)S(1)}, u32[]{:S(2)}, u32[]{:S(2)}) collective-permute-start(bf16[512,128]{1,0:T(8,128)(2,1)} %param.21), channel_id=1, source_target_pairs={{48,0},{0,16},{16,32},{32,48},{49,1},{1,17},{17,33},{33,49},{50,2}... | collective-permute-start | bytes 393224 | tf_op jit(solution)/shard_map/ppermute | solution.py:170
  12.3 11.1 %copy-start.5 = (bf16[512,128]{1,0:T(8,128)(2,1)S(1)}, bf16[512,128]{1,0:T(8,128)(2,1)}, u32[]{:S(2)}) copy-start(bf16[512,128]{1,0:T(8,128)(2,1)} %param.21) | copy-start | bytes 393220
  12.3 24.3 %all-to-all-start = ((bf16[64,4,512]{2,1,0:T(4,128)(2,1)}), bf16[64,4,512]{2,1,0:T(4,128)(2,1)S(1)}, u32[]{:S(2)}, u32[]{:S(2)}) async-start(bf16[64,4,512]{2,1,0:T(4,128)(2,1)} %broadcast_in_dim.14), calls=%async_computation | async-start | bytes 524288 | tf_op jit(solution)/shard_map/all_to_all | solution.py:159
  24.1 0.8 copy-start.8
  25.5 0.7 copy-start.9
  25.5 0.7 copy-start.10
  25.5 1.1 %copy-start.7 = (bf16[256,512]{1,0:T(8,128)(2,1)S(1)}, bf16[256,512]{1,0:T(8,128)(2,1)}, u32[]{:S(2)}) copy-start(bf16[256,512]{1,0:T(8,128)(2,1)} %param.11) | copy-start | bytes 786436
  26.8 1.0 %copy-start.1 = (bf16[4,512,128]{2,1,0:T(8,128)(2,1)S(1)}, bf16[4,512,128]{2,1,0:T(8,128)(2,1)}, u32[]{:S(2)}) copy-start(bf16[4,512,128]{2,1,0:T(8,128)(2,1)} %v_ref.3) | copy-start | bytes 1572868
  27.0 1.1 %copy-start = (bf16[4,512,128]{2,1,0:T(8,128)(2,1)S(1)}, bf16[4,512,128]{2,1,0:T(8,128)(2,1)}, u32[]{:S(2)}) copy-start(bf16[4,512,128]{2,1,0:T(8,128)(2,1)} %k_ref.1) | copy-start | bytes 1572868
  27.2 0.9 copy-start.3
  27.3 0.8 copy-start.4
  34.2 2.4 %copy-start.2 = (bf16[256,128]{1,0:T(8,128)(2,1)S(1)}, bf16[256,128]{1,0:T(8,128)(2,1)}, u32[]{:S(2)}) copy-start(bf16[256,128]{1,0:T(8,128)(2,1)} %v_ref.2) | copy-start | bytes 196612
  34.2 13.2 %copy-start.6 = (bf16[8,512,128]{2,1,0:T(8,128)(2,1)S(1)}, bf16[8,512,128]{2,1,0:T(8,128)(2,1)}, u32[]{:S(2)}) copy-start(bf16[8,512,128]{2,1,0:T(8,128)(2,1)} %bitcast_dynamic-update-slice_fusion.7) | copy-start | bytes 3145732
  38.7 20.4 %all-to-all-start.1 = ((bf16[64,2,640]{2,1,0:T(2,128)(2,1)}), bf16[64,2,640]{2,1,0:T(2,128)(2,1)S(1)}, u32[]{:S(2)}, u32[]{:S(2)}) async-start(bf16[64,2,640]{2,1,0:T(2,128)(2,1)} %reshape.170), calls=%async_computation.1 | async-start | bytes 327680 | tf_op jit(solution)/shard_map/all_to_all | solution.py:212
  60.2 11.5 %all-to-all-start.2 = ((bf16[16,4,512]{2,1,0:T(4,128)(2,1)}), bf16[16,4,512]{2,1,0:T(4,128)(2,1)S(1)}, u32[]{:S(2)}, u32[]{:S(2)}) async-start(bf16[16,4,512]{2,1,0:T(4,128)(2,1)} %shard_map.124), calls=%async_computation.2 | async-start | bytes 131072 | tf_op jit(solution)/shard_map/all_to_all | solution.py:220
  72.6 20.0 %all-to-all-start.3 = ((bf16[32,8,128]{2,1,0:T(8,128)(2,1)}), bf16[32,8,128]{2,1,0:T(8,128)(2,1)S(1)}, u32[]{:S(2)}, u32[]{:S(2)}) async-start(bf16[32,8,128]{2,1,0:T(8,128)(2,1)} %bitcast.22), calls=%async_computation.3 | async-start | bytes 131072 | tf_op jit(solution)/shard_map/all_to_all | solution.py:225

commit v3 on v2

--- a/solution.py
+++ b/solution.py
@@ -22,21 +22,13 @@
 vmem_limit = 32 * 1024 * 1024
 
 
-def rotate(values, positions):
-    half_dim = values.shape[-1] // 2
-    frequency = rope_base ** (-2.0 * jnp.arange(half_dim, dtype=f32) / values.shape[-1])
+def angles(offset, row_count):
+    lane = jnp.arange(HD, dtype=jnp.int32)
+    frequency = rope_base ** (-2.0 * (lane % (HD // 2)).astype(f32) / HD)
+    positions = offset + jnp.arange(row_count, dtype=jnp.int32)
     angle_rad = positions.astype(f32)[:, None] * frequency[None, :]
-    cosine = jnp.cos(angle_rad)[:, None, :]
-    sine_part = jnp.sin(angle_rad)[:, None, :]
-    lower_half = values[..., :half_dim]
-    upper_half = values[..., half_dim:]
-    return jnp.concatenate(
-        [
-            lower_half * cosine - upper_half * sine_part,
-            upper_half * cosine + lower_half * sine_part,
-        ],
-        axis=-1,
-    )
+    sign = jnp.where(lane < HD // 2, -1.0, 1.0)
+    return jnp.cos(angle_rad), jnp.sin(angle_rad) * sign[None, :]
 
 
 def dot(a, b, dims):
@@ -53,6 +45,27 @@
         out_shape=outs,
         compiler_params=pltpu.CompilerParams(vmem_limit_bytes=vmem_limit),
     )(*args)
+
+
+def prefill_kernel(q_ref, k_ref, v_ref, cos_ref, sin_ref, out_ref, key_ref):
+    rows = k_ref.shape[0]
+    cosine, sine_part = cos_ref[...], sin_ref[...]
+
+    def rotate(values):
+        values = values.astype(f32)
+        turned = pltpu.roll(values, HD // 2, 1)
+        return (values * cosine + turned * sine_part).astype(bf16)
+
+    keys = rotate(k_ref[...])
+    key_ref[...] = keys
+    causal = iota((rows, rows), 1) <= iota((rows, rows), 0)
+    for h in range(QPK):
+        part = slice(h * HD, (h + 1) * HD)
+        scores = dot(rotate(q_ref[:, part]), keys, ((1,), (1,))) * scale
+        scores = jnp.where(causal, scores, neg_large)
+        weights = jnp.exp(scores - jnp.max(scores, axis=1, keepdims=True))
+        weights = weights * (1.0 / jnp.sum(weights, axis=1, keepdims=True))
+        out_ref[:, part] = dot(weights.astype(bf16), v_ref[...], ((1,), (0,))).astype(bf16)
 
 
 def resident_kernel(q_ref, k_ref, v_ref, len_ref, sum_ref, peak_ref, total_ref):
@@ -79,6 +92,10 @@
     total_ref[...] = jnp.broadcast_to(total, (ROWS, HD))
 
 
+def repeat_kernel(q_ref, out_ref):
+    out_ref[...] = jnp.broadcast_to(q_ref[...][None], out_ref.shape)
+
+
 def parts_of(value, count):
     parts = []
     for _ in range(count):
@@ -107,8 +124,9 @@
         for block, part in enumerate(parts_of(peak, 3) + parts_of(total, 2)):
             extra = jnp.where(lane // REQ == block * QPK + h, part, extra)
     payload = jnp.concatenate(columns + [extra], axis=1).astype(bf16)
-    placing = (iota((pages, out_ref.shape[0]), 1) == slot_ref[...]).astype(f32).astype(bf16)
-    out_ref[...] = dot(placing, payload, ((0,), (0,))).astype(bf16)
+    placing = (iota((pages, out_ref.shape[0] * CAP), 1) == slot_ref[...]).astype(f32).astype(bf16)
+    placed = dot(placing, payload, ((0,), (0,)))
+    out_ref[...] = placed.reshape(out_ref.shape).astype(bf16)
 
 
 def combine_kernel(got_ref, sum_ref, peak_ref, total_ref, out_ref):
@@ -138,6 +156,20 @@
     out_ref[...] = jnp.broadcast_to(wide[None], out_ref.shape).astype(bf16)
 
 
+def sum_kernel(terms_ref, out_ref):
+    half = terms_ref.shape[0] // 2
+    sums = []
+    for c in range(2):
+        total = terms_ref[c * half].astype(f32)
+        for t in range(1, half):
+            total = total + terms_ref[c * half + t].astype(f32)
+        sums.append(total)
+    blocks = []
+    for x in range(terms_ref.shape[1] // REQ):
+        blocks += [sums[c][x * REQ : (x + 1) * REQ] for c in range(2)]
+    out_ref[...] = jnp.concatenate(blocks, axis=0).astype(bf16)
+
+
 def on_device(
     prefill_q,
     prefill_k,
@@ -157,33 +189,34 @@
     width = decode_q.shape[1]
 
     asked = lax.all_to_all(
-        jnp.broadcast_to(decode_q[None], (groups,) + decode_q.shape),
+        call(repeat_kernel, jax.ShapeDtypeStruct((groups,) + decode_q.shape, bf16), decode_q),
         grp,
         split_axis=0,
         concat_axis=0,
         tiled=True,
     ).reshape(groups * REQ, width)
 
-    steps = lax.axis_size("x")
-    here = lax.axis_index("x")
-    pieces = [out_weight] + [
-        lax.ppermute(out_weight, "x", [((i + k) % steps, i) for i in range(steps)])
-        for k in range(1, steps)
-    ]
-    columns = jnp.roll(jnp.stack(pieces), here, axis=0)
-
-    positions = span_offset[0] + jnp.arange(row_count, dtype=jnp.int32)
-    key_rot = rotate(prefill_k.astype(f32).reshape(row_count, 1, HD), positions).astype(bf16)
-    query_rot = rotate(prefill_q.astype(f32).reshape(row_count, QPK, HD), positions).astype(bf16)
-    scores = jnp.einsum("qgd,sd->gqs", query_rot, key_rot[:, 0], preferred_element_type=f32) * scale
-    place = jnp.arange(row_count, dtype=jnp.int32)
-    scores = jnp.where(place[None, :] <= place[:, None], scores, neg_large)
-    weights = jnp.exp(scores - jnp.max(scores, axis=-1, keepdims=True))
-    weights_low = (weights / jnp.sum(weights, axis=-1, keepdims=True)).astype(bf16)
-    prefill_out = (
-        jnp.einsum("gqs,sd->qgd", weights_low, prefill_v, preferred_element_type=f32)
-        .astype(bf16)
-        .reshape(row_count, QPK * HD)
+    cosine, sine_part = angles(span_offset[0], row_count)
+    prefill_out, key_rot = call(
+        prefill_kernel,
+        (
+            jax.ShapeDtypeStruct(prefill_q.shape, bf16),
+            jax.ShapeDtypeStruct(prefill_k.shape, bf16),
+        ),
+        prefill_q,
+        prefill_k,
+        prefill_v,
+        cosine,
+        sine_part,
+    )
+    key_rot, own_weight = lax.optimization_barrier((key_rot, out_weight))
+    other_weight = lax.ppermute(own_weight, "c", [(0, 1), (1, 0)])
+    first = lax.axis_index("c") == 0
+    columns = jnp.stack(
+        [
+            jnp.where(first, own_weight, other_weight),
+            jnp.where(first, other_weight, own_weight),
+        ]
     )
 
     target = page_group[:, 0]
@@ -199,32 +232,36 @@
     home = call(
         resident_kernel, (rows_of,) * 3, decode_q, cache_k, cache_v, cache_len.reshape(1, REQ)
     )
+    asked, prefill_out, columns, home = lax.optimization_barrier(
+        (asked, prefill_out, columns, home)
+    )
     sent = call(
         page_kernel,
-        jax.ShapeDtypeStruct((groups * CAP, width + HD), bf16),
+        jax.ShapeDtypeStruct((groups, CAP, width + HD), bf16),
         asked,
-        key_rot[:, 0],
+        key_rot,
         prefill_v,
         owner,
         slot_index,
         (page_request + 1)[:, None],
     )
-    got = lax.all_to_all(
-        sent.reshape(groups, CAP, width + HD), grp, split_axis=0, concat_axis=0, tiled=True
-    ).reshape(groups * CAP, width + HD)
-
-    peers = lax.axis_size(("y", "c"))
+    got = lax.all_to_all(sent, grp, split_axis=0, concat_axis=0, tiled=True)
+    got = got.reshape(groups * CAP, width + HD)
+
+    peers = lax.axis_size(("y", "x"))
     repeated = call(
         combine_kernel, jax.ShapeDtypeStruct((peers, REQ, width), bf16), got, *home
     )
-    everyone = lax.all_to_all(repeated, ("y", "c"), split_axis=0, concat_axis=0, tiled=True)
+    everyone = lax.all_to_all(repeated, ("y", "x"), split_axis=0, concat_axis=0, tiled=True)
     everyone = everyone.reshape(peers * REQ, width)
     shards = lax.axis_size("z")
-    terms = jnp.einsum("ad,xdc->xac", everyone, columns, preferred_element_type=f32).astype(bf16)
-    terms = terms.reshape(steps * shards, peers * REQ // shards, HD)
-    terms = lax.all_to_all(terms, ("x", "z"), split_axis=0, concat_axis=0, tiled=True)
-    terms = terms.reshape(steps, shards, peers * REQ // shards, HD)
-    decode_out = jnp.sum(terms.astype(f32), axis=1).astype(bf16).reshape(-1, HD)
+    cores = lax.axis_size("c")
+    terms = jnp.einsum("ad,cde->cae", everyone, columns, preferred_element_type=f32).astype(bf16)
+    terms = terms.reshape(cores * shards, peers * REQ // shards, HD)
+    terms = lax.all_to_all(terms, ("c", "z"), split_axis=0, concat_axis=0, tiled=True)
+    decode_out = call(
+        sum_kernel, jax.ShapeDtypeStruct((peers * REQ * cores // shards, HD), bf16), terms
+    )
     return (prefill_out, decode_out)
 
 

time: 93.8 us -> 78.2 us (0.83)
  blocking collectives: 0 us -> 48.1 us
  starting transfers between devices: 44.8 us -> 14.1 us
  waiting for transfers between devices: 27.6 us -> 5.18 us
  local copies, waits for them, and re-layouts: 11.9 us -> 2.44 us
  Pallas kernels: 2.87 us -> 5.58 us
  matrix products: 2.21 us -> 0.19 us
  other arithmetic: 2.2 us -> 0.8 us
    all_to_all x0 -> x3, blocking collectives: none -> 48.1 us  [the longest x1 19.4 us: on_device(): lax.all_to_all(terms, ('c', 'z'), split_axis=0, concat_axis=0, tiled=True)]
    all_to_all x4 -> x1, starting transfers between devices: 34.6 us -> 11.8 us  [on_device(): lax.all_to_all(call(repeat_kernel, jax.ShapeDtypeStruct((groups,) + decod...]
    all_to_all x4 -> x1, waiting for transfers between devices: 27.6 us -> 5.17 us  [on_device(): lax.all_to_all(call(repeat_kernel, jax.ShapeDtypeStruct((groups,) + decod...]
    ppermute x3 -> x1, starting transfers between devices: 10.2 us -> 2.35 us  [on_device(): other_weight = lax.ppermute(own_weight, 'c', [(0, 1), (1, 0)])]
    unnamed x33 -> x22, local copies, waits for them, and re-layouts: 9.28 us -> 2.02 us
    pallas_call x3 -> x6, Pallas kernels: 2.87 us -> 5.58 us  [call(): pl.pallas_call(kernel, out_shape=outs, compiler_params=pltpu.CompilerPara...]
    broadcast_in_dim x1 -> x0, local copies, waits for them, and re-layouts: 1.46 us -> none  [on_device(): jnp.broadcast_to(decode_q[None], (groups,) + decode_q.shape)]
    dot_general x3 -> x1, matrix products: 1.64 us -> 0.19 us  [on_device(): jnp.einsum('ad,cde->cae', everyone, columns, preferred_element_type=f32)]
  transfers between devices with their start and end apart: 7 -> 2, of which waited for: 4 -> 1; matrix products, arithmetic and copies ran while one was open for 14% -> 1% of each run, Pallas kernels for 1% -> 3%
where the time goes in v3:
time: 78.2 us; the launch traced here: 77.9 us
  blocking collectives  48.1 us (62%)
  starting transfers between devices  14.1 us (18%)
  Pallas kernels  5.58 us (7%)
  waiting for transfers between devices  5.18 us (7%)
  local copies, waits for them, and re-layouts  2.44 us (3%)
  between operations  1.51 us (2%)
  other arithmetic  0.8 us (1%)
    all_to_all x1, blocking collectives, on_device(): lax.all_to_all(terms, ('c', 'z'), split_axis=0, concat_axis=0, tiled=True)  19.4 us
    all_to_all x1, blocking collectives, on_device(): got = lax.all_to_all(sent, grp, split_axis=0, concat_axis=0, tiled=True)  16.3 us
    all_to_all x1, blocking collectives, on_device(): lax.all_to_all(repeated, ('y', 'x'), split_axis=0, concat_axis=0, tiled=T...  12.3 us
    all_to_all x1, starting transfers between devices, on_device(): lax.all_to_all(call(repeat_kernel, jax.ShapeDtypeStruct((groups,) + decod...  11.8 us
    pallas_call x6, Pallas kernels, call(): pl.pallas_call(kernel, out_shape=outs, compiler_params=pltpu.CompilerPara...  5.58 us
    all_to_all x1, waiting for transfers between devices, on_device(): lax.all_to_all(call(repeat_kernel, jax.ShapeDtypeStruct((groups,) + decod...  5.17 us
    ppermute x1, starting transfers between devices, on_device(): other_weight = lax.ppermute(own_weight, 'c', [(0, 1), (1, 0)])  2.35 us
    unnamed x22, local copies, waits for them, and re-layouts  2.02 us
  transfers between devices with their start and end apart: 2, of which 1 were waited for; matrix products, arithmetic and copies ran while one was open for 1% of the time, Pallas kernels for 3%

profile of v3, /device:TPU:1, one launch (start us, length us, event | category | flops | bytes accessed | tf_op | source)
XLA Modules:
  0.0 77.9 jit_solution(2947660784983307431)
XLA Ops:
  0.6 0.0 copy-start.5
  0.6 0.7 copy-done.5
  1.3 0.0 copy-start.3
  1.3 0.7 shard_map.122
  2.0 0.0 copy-start.2
  2.0 0.0 copy-start.4
  2.0 0.0 copy-start.1
  2.0 11.8 %all-to-all-start = ((bf16[64,4,512]{2,1,0:T(4,128)(2,1)}), bf16[64,4,512]{2,1,0:T(4,128)(2,1)S(1)}, u32[]{:S(2)}, u32[]{:S(2)}) async-start(bf16[64,4,512]{2,1,0:T(4,128)(2,1)} %shard_map.122), calls=%async_computation | async-start | bytes 524288 | tf_op jit(solution)/shard_map/all_to_all | solution.py:191
  13.8 0.0 copy-start
  14.5 0.5 fusion
  15.1 0.0 copy-done.3
  15.1 0.0 copy-done.2
  15.1 0.0 copy-done.4
  15.1 0.0 copy-start.8
  15.1 1.9 %shard_map.123 = (bf16[256,512]{1,0:T(8,128)(2,1)}, bf16[256,128]{1,0:T(8,128)(2,1)S(1)}) custom-call(bf16[256,512]{1,0:T(8,128)(2,1)S(1)} %copy-done.3, bf16[256,128]{1,0:T(8,128)(2,1)S(1)} %copy-done.4, bf16[256,128]{1,0:T(8,128)(2,1)S(1)} %copy-done.2, f32[256,128]{1,0:T(8,128)S(1)} %get-tuple-element.31.cos_ref, f32[256,128]{1,0:T(8,128)S(1)} %get-tuple-element.30.sin_ref), custom_call_target="tpu_custom_call" | custom-call | tf_op jit(solution)/shard_map/pallas_call | solution.py:43
  17.0 0.0 copy-done.8
  17.0 2.4 %collective-permute-start = (bf16[512,128]{1,0:T(8,128)(2,1)S(1)}, bf16[512,128]{1,0:T(8,128)(2,1)S(1)}, u32[]{:S(2)}, u32[]{:S(2)}) collective-permute-start(bf16[512,128]{1,0:T(8,128)(2,1)S(1)} %copy-done.8), channel_id=1, source_target_pairs={{0,8},{8,0},{1,9},{9,1},{2,10},{10,2},{3,11},{11,3},{4,12},{12,4},... | collective-permute-start | bytes 393224 | tf_op jit(solution)/shard_map/ppermute | solution.py:213
  19.4 0.0 copy-start.9
  19.4 0.0 copy-start.10
  19.4 0.6 copy-done.9
  20.0 0.0 copy-done.10
  20.1 0.1 copy.23.owner_ref
  20.2 0.2 convert_reduce_fusion
  20.3 0.1 copy.24.slot_ref
  20.4 0.0 copy-start.6
  20.4 0.1 copy.25.place_ref
  20.5 0.0 copy-start.7
  20.5 0.0 copy-done.1
  20.5 0.0 copy-done
  20.5 0.6 copy-done.6
  21.1 0.1 copy-done.7
  21.2 0.5 shard_map.124
  21.7 0.0 collective-permute-done
  21.8 5.2 %all-to-all-done = bf16[64,4,512]{2,1,0:T(4,128)(2,1)S(1)} async-done(((bf16[64,4,512]{2,1,0:T(4,128)(2,1)}), bf16[64,4,512]{2,1,0:T(4,128)(2,1)S(1)}, u32[]{:S(2)}, u32[]{:S(2)}) %all-to-all-start) | async-done | bytes 262176 | tf_op jit(solution)/shard_map/all_to_all | solution.py:191
  27.0 0.1 reshape.43.q_ref
  27.0 1.5 %shard_map.125 = bf16[64,2,640]{2,1,0:T(2,128)(2,1)S(1)} custom-call(bf16[256,512]{1,0:T(8,128)(2,1)S(1)} %reshape.43.q_ref, bf16[256,128]{1,0:T(8,128)(2,1)S(1)} %get-tuple-element.24.k_ref, bf16[256,128]{1,0:T(8,128)(2,1)S(1)} %copy-done.2, s32[16,1]{1,0:T(8,128)S(1)} %copy.23.owner_ref, s32[16,1]{1,0:T(8,128)S(1)} %copy.24.slot_ref, ...), custom_call_target="tpu_custom_call" | custom-call | tf_op jit(solution)/shard_map/pallas_call | solution.py:43
  28.5 16.3 %all_to_all.20 = bf16[64,2,640]{2,1,0:T(2,128)(2,1)S(1)} all-to-all(bf16[64,2,640]{2,1,0:T(2,128)(2,1)S(1)} %shard_map.125), channel_id=1, replica_groups=mesh['y'=8,'x'=4,'c'=2,'z'=8] {'y','x','c'}, dimensions={0} | all-to-all | bytes 327680 | tf_op jit(solution)/shard_map/all_to_all | solution.py:248
  44.9 0.1 reshape.45.got_ref
  44.9 0.3 shard_map.126
  45.3 12.3 %all_to_all.21 = bf16[32,4,512]{2,1,0:T(4,128)(2,1)S(1)} all-to-all(bf16[32,4,512]{2,1,0:T(4,128)(2,1)S(1)} %shard_map.126), channel_id=1, replica_groups=mesh['y'=8,'x'=4,'c'=2,'z'=8] {'y','x'}, dimensions={0} | all-to-all | bytes 262144 | tf_op jit(solution)/shard_map/all_to_all | solution.py:255
  57.7 0.2 convolution_convert_fusion
  57.9 19.4 %all_to_all.22.terms_ref = bf16[16,16,128]{2,1,0:T(8,128)(2,1)S(1)} all-to-all(bf16[16,16,128]{2,1,0:T(8,128)(2,1)S(1)} %bitcast.21), channel_id=1, replica_groups=mesh['y'=8,'x'=4,'c'=2,'z'=8] {'c','z'}, dimensions={0} | all-to-all | bytes 131072 | tf_op jit(solution)/shard_map/all_to_all | solution.py:261
  77.2 0.6 shard_map.127
  (7 shorter events, 0.1 us)
Async XLA Ops:
  0.6 0.7 copy-start.5
  1.3 13.8 %copy-start.3 = (bf16[256,512]{1,0:T(8,128)(2,1)S(1)}, bf16[256,512]{1,0:T(8,128)(2,1)}, u32[]{:S(2)}) copy-start(bf16[256,512]{1,0:T(8,128)(2,1)} %q_ref.4) | copy-start | bytes 786436
  2.0 13.1 %copy-start.2 = (bf16[256,128]{1,0:T(8,128)(2,1)S(1)}, bf16[256,128]{1,0:T(8,128)(2,1)}, u32[]{:S(2)}) copy-start(bf16[256,128]{1,0:T(8,128)(2,1)} %v_ref.5) | copy-start | bytes 196612
  2.0 13.1 %copy-start.4 = (bf16[256,128]{1,0:T(8,128)(2,1)S(1)}, bf16[256,128]{1,0:T(8,128)(2,1)}, u32[]{:S(2)}) copy-start(bf16[256,128]{1,0:T(8,128)(2,1)} %k_ref.2) | copy-start | bytes 196612
  2.0 18.5 %copy-start.1 = (bf16[4,512,128]{2,1,0:T(8,128)(2,1)S(1)}, bf16[4,512,128]{2,1,0:T(8,128)(2,1)}, u32[]{:S(2)}) copy-start(bf16[4,512,128]{2,1,0:T(8,128)(2,1)} %v_ref.4) | copy-start | bytes 1572868
  2.0 24.9 %all-to-all-start = ((bf16[64,4,512]{2,1,0:T(4,128)(2,1)}), bf16[64,4,512]{2,1,0:T(4,128)(2,1)S(1)}, u32[]{:S(2)}, u32[]{:S(2)}) async-start(bf16[64,4,512]{2,1,0:T(4,128)(2,1)} %shard_map.122), calls=%async_computation | async-start | bytes 524288 | tf_op jit(solution)/shard_map/all_to_all | solution.py:191
  13.8 6.7 %copy-start = (bf16[4,512,128]{2,1,0:T(8,128)(2,1)S(1)}, bf16[4,512,128]{2,1,0:T(8,128)(2,1)}, u32[]{:S(2)}) copy-start(bf16[4,512,128]{2,1,0:T(8,128)(2,1)} %k_ref.3) | copy-start | bytes 1572868
  15.1 1.9 %copy-start.8 = (bf16[512,128]{1,0:T(8,128)(2,1)S(1)}, bf16[512,128]{1,0:T(8,128)(2,1)}, u32[]{:S(2)}) copy-start(bf16[512,128]{1,0:T(8,128)(2,1)} %param.21) | copy-start | bytes 393220
  17.0 4.7 %collective-permute-start = (bf16[512,128]{1,0:T(8,128)(2,1)S(1)}, bf16[512,128]{1,0:T(8,128)(2,1)S(1)}, u32[]{:S(2)}, u32[]{:S(2)}) collective-permute-start(bf16[512,128]{1,0:T(8,128)(2,1)S(1)} %copy-done.8), channel_id=1, source_target_pairs={{0,8},{8,0},{1,9},{9,1},{2,10},{10,2},{3,11},{11,3},{4,12},{12,4},... | collective-permute-start | bytes 393224 | tf_op jit(solution)/shard_map/ppermute | solution.py:213
  19.4 0.7 copy-start.9
  19.4 0.7 copy-start.10
  20.4 0.7 copy-start.6
  20.5 0.7 copy-start.7

commit v4 on v3

--- a/solution.py
+++ b/solution.py
@@ -20,6 +20,9 @@
 f32 = jnp.float32
 bf16 = jnp.bfloat16
 vmem_limit = 32 * 1024 * 1024
+shadow_flops = 5 * 10**9
+CH = 256
+at_values, at_info, at_weight, at_end = CH, 2 * CH, 2 * CH + 16, 2 * CH + 16 + 512
 
 
 def angles(offset, row_count):
@@ -39,33 +42,56 @@
     return lax.broadcasted_iota(jnp.int32, shape, axis)
 
 
-def call(kernel, outs, *args):
+def call(kernel, outs, *args, scalars=0, unread=0, flops=0):
+    moved = sum(a.size * a.dtype.itemsize for a in (*args, *jax.tree.leaves(outs)))
+    places = [pltpu.SMEM] * scalars + [pltpu.VMEM] * (len(args) - scalars - unread)
+    places += [pl.ANY] * unread
     return pl.pallas_call(
         kernel,
         out_shape=outs,
+        in_specs=[pl.BlockSpec(memory_space=place) for place in places],
+        cost_estimate=pl.CostEstimate(flops=flops, bytes_accessed=moved, transcendentals=0),
         compiler_params=pltpu.CompilerParams(vmem_limit_bytes=vmem_limit),
     )(*args)
 
 
-def prefill_kernel(q_ref, k_ref, v_ref, cos_ref, sin_ref, out_ref, key_ref):
-    rows = k_ref.shape[0]
+def rotate(values, cosine, sine_part):
+    values = values.astype(f32)
+    return (values * cosine + pltpu.roll(values, HD // 2, 1) * sine_part).astype(bf16)
+
+
+def pack_kernel(
+    k_ref, v_ref, cos_ref, sin_ref, group_ref, request_ref, weight_ref, _, pack_ref
+):
+    pack_ref[:at_values, :] = rotate(k_ref[...], cos_ref[...], sin_ref[...])
+    pack_ref[at_values:at_info, :] = v_ref[...]
+    pack_ref[at_weight:, :] = weight_ref[...]
+
+    pages = group_ref.shape[1]
+    eye = iota((pages, pages), 0) == iota((pages, pages), 1)
+    group_row = group_ref[...].astype(f32)
+    group = jnp.sum(jnp.where(eye, group_row, 0.0), axis=1, keepdims=True)
+    request = jnp.sum(jnp.where(eye, request_ref[...].astype(f32), 0.0), axis=1, keepdims=True)
+    before = iota((pages, pages), 1) < iota((pages, pages), 0)
+    earlier = jnp.where(before & (group == group_row), 1.0, 0.0)
+    earlier = jnp.sum(earlier, axis=1, keepdims=True)
+    lane = iota((pages, HD), 1)
+    info = jnp.where(lane == 0, group, jnp.where(lane == 1, request, earlier))
+    pack_ref[at_info:at_weight, :] = info.astype(bf16)
+
+
+def prefill_kernel(q_ref, pack_ref, cos_ref, sin_ref, _, out_ref):
     cosine, sine_part = cos_ref[...], sin_ref[...]
-
-    def rotate(values):
-        values = values.astype(f32)
-        turned = pltpu.roll(values, HD // 2, 1)
-        return (values * cosine + turned * sine_part).astype(bf16)
-
-    keys = rotate(k_ref[...])
-    key_ref[...] = keys
-    causal = iota((rows, rows), 1) <= iota((rows, rows), 0)
+    keys, values = pack_ref[:at_values, :], pack_ref[at_values:at_info, :]
+    causal = iota((CH, CH), 1) <= iota((CH, CH), 0)
     for h in range(QPK):
         part = slice(h * HD, (h + 1) * HD)
-        scores = dot(rotate(q_ref[:, part]), keys, ((1,), (1,))) * scale
+        queries = rotate(q_ref[:, part], cosine, sine_part)
+        scores = dot(queries, keys, ((1,), (1,))) * scale
         scores = jnp.where(causal, scores, neg_large)
         weights = jnp.exp(scores - jnp.max(scores, axis=1, keepdims=True))
         weights = weights * (1.0 / jnp.sum(weights, axis=1, keepdims=True))
-        out_ref[:, part] = dot(weights.astype(bf16), v_ref[...], ((1,), (0,))).astype(bf16)
+        out_ref[:, part] = dot(weights.astype(bf16), values, ((1,), (0,))).astype(bf16)
 
 
 def resident_kernel(q_ref, k_ref, v_ref, len_ref, sum_ref, peak_ref, total_ref):
@@ -105,28 +131,51 @@
     return parts
 
 
-def page_kernel(q_ref, k_ref, v_ref, owner_ref, slot_ref, place_ref, out_ref):
-    pages = owner_ref.shape[0]
-    tokens = k_ref.shape[0]
-    chosen = (iota((pages, q_ref.shape[0]), 1) == owner_ref[...]).astype(f32).astype(bf16)
-    queries = dot(chosen, q_ref[...], ((1,), (0,))).astype(bf16)
-    own = (iota((pages, tokens), 1) // PAGE) == iota((pages, tokens), 0)
+def page_kernel(core_ref, q_ref, own_ref, other_ref, out_ref):
+    core = core_ref[0].astype(f32)
+    pages = at_weight - at_info
+    slots = out_ref.shape[0] * out_ref.shape[1]
+    placed = jnp.zeros((slots, out_ref.shape[2]), f32)
+    own = iota((QPK * pages, CH), 1) // PAGE == iota((QPK * pages, CH), 0) % pages
     lane = iota((pages, HD), 1)
-    extra = jnp.where(lane // ROWS == 5, place_ref[...].astype(f32), 0.0)
-    columns = []
-    for h in range(QPK):
-        scores = dot(queries[:, h * HD : (h + 1) * HD], k_ref[...], ((1,), (1,))) * scale
+    row_lane = iota((pages, q_ref.shape[0]), 1).astype(f32)
+    slot_lane = iota((pages, slots), 1).astype(f32)
+    for side, ref in enumerate((own_ref, other_ref)):
+        info = ref[at_info:at_weight, :].astype(f32)
+        group, request, earlier = info[:, 0:1], info[:, 1:2], info[:, 2:3]
+        chip = jnp.floor(group * 0.5)
+        mine = group - 2.0 * chip == core
+        row = jnp.where(mine, chip * REQ + request, -1.0)
+        slot = jnp.where(mine, chip * (2 * CAP) + side * CAP + earlier, -1.0)
+        chosen = (row_lane == row).astype(f32).astype(bf16)
+        placing = (slot_lane == slot).astype(f32).astype(bf16)
+        asked = dot(chosen, q_ref[...], ((1,), (0,)))
+        asked = [asked[:, h * HD : (h + 1) * HD] for h in range(QPK)]
+        queries = jnp.concatenate(asked, axis=0).astype(bf16)
+        scores = dot(queries, ref[:at_values, :], ((1,), (1,))) * scale
         scores = jnp.where(own, scores, neg_large)
         peak = jnp.max(scores, axis=1, keepdims=True)
         weights = jnp.where(own, jnp.exp(scores - peak), 0.0)
         total = jnp.sum(weights, axis=1, keepdims=True)
-        columns.append(dot(weights.astype(bf16), v_ref[...], ((1,), (0,))) / total)
-        for block, part in enumerate(parts_of(peak, 3) + parts_of(total, 2)):
-            extra = jnp.where(lane // REQ == block * QPK + h, part, extra)
-    payload = jnp.concatenate(columns + [extra], axis=1).astype(bf16)
-    placing = (iota((pages, out_ref.shape[0] * CAP), 1) == slot_ref[...]).astype(f32).astype(bf16)
-    placed = dot(placing, payload, ((0,), (0,)))
+        values = dot(weights.astype(bf16), ref[at_values:at_info, :], ((1,), (0,))) / total
+        extra = jnp.where(lane // ROWS == 5, request + 1.0, 0.0)
+        parts = parts_of(peak, 3) + parts_of(total, 2)
+        columns = []
+        for h in range(QPK):
+            part = slice(h * pages, (h + 1) * pages)
+            columns.append(values[part])
+            for block, column in enumerate(parts):
+                extra = jnp.where(lane // REQ == block * QPK + h, column[part], extra)
+        payload = jnp.concatenate(columns + [extra], axis=1).astype(bf16)
+        placed = placed + dot(placing, payload, ((0,), (0,)))
     out_ref[...] = placed.reshape(out_ref.shape).astype(bf16)
+
+
+def project_kernel(core_ref, rows_ref, own_ref, other_ref, out_ref):
+    core = core_ref[0]
+    for index, ref in ((core, own_ref), (1 - core, other_ref)):
+        product = dot(rows_ref[...], ref[at_weight:, :], ((1,), (0,)))
+        out_ref[index] = product.astype(bf16)
 
 
 def combine_kernel(got_ref, sum_ref, peak_ref, total_ref, out_ref):
@@ -183,81 +232,76 @@
     cache_len,
     out_weight,
 ):
-    grp = ("y", "x", "c")
-    groups = lax.axis_size(grp)
-    row_count = prefill_q.shape[0]
+    chips = ("y", "x")
+    peers = lax.axis_size(chips)
     width = decode_q.shape[1]
 
-    asked = lax.all_to_all(
-        call(repeat_kernel, jax.ShapeDtypeStruct((groups,) + decode_q.shape, bf16), decode_q),
-        grp,
-        split_axis=0,
-        concat_axis=0,
-        tiled=True,
-    ).reshape(groups * REQ, width)
-
-    cosine, sine_part = angles(span_offset[0], row_count)
-    prefill_out, key_rot = call(
-        prefill_kernel,
-        (
-            jax.ShapeDtypeStruct(prefill_q.shape, bf16),
-            jax.ShapeDtypeStruct(prefill_k.shape, bf16),
-        ),
-        prefill_q,
+    asking = call(repeat_kernel, jax.ShapeDtypeStruct((peers,) + decode_q.shape, bf16), decode_q)
+    asked = lax.all_to_all(asking, chips, split_axis=0, concat_axis=0, tiled=True)
+    asked = asked.reshape(peers * REQ, width)
+
+    core = lax.axis_index("c").reshape(1)
+    cosine, sine_part = angles(span_offset[0], prefill_q.shape[0])
+    own = call(
+        pack_kernel,
+        jax.ShapeDtypeStruct((at_end, HD), bf16),
         prefill_k,
         prefill_v,
         cosine,
         sine_part,
-    )
-    key_rot, own_weight = lax.optimization_barrier((key_rot, out_weight))
-    other_weight = lax.ppermute(own_weight, "c", [(0, 1), (1, 0)])
-    first = lax.axis_index("c") == 0
-    columns = jnp.stack(
-        [
-            jnp.where(first, own_weight, other_weight),
-            jnp.where(first, other_weight, own_weight),
-        ]
-    )
-
-    target = page_group[:, 0]
-    page_index = jnp.arange(target.shape[0], dtype=jnp.int32)
-    same_target = target[None, :] == target[:, None]
-    earlier = jnp.sum(
-        (same_target & (page_index[None, :] < page_index[:, None])).astype(jnp.int32), axis=1
-    )
-    slot_index = (target * CAP + earlier)[:, None]
-    owner = (target * REQ + page_request)[:, None]
+        page_group.reshape(1, -1),
+        page_request.reshape(1, -1),
+        out_weight,
+        asking,
+        unread=1,
+    )
+    other = lax.ppermute(own, "c", [(0, 1), (1, 0)])
 
     rows_of = jax.ShapeDtypeStruct((ROWS, HD), f32)
     home = call(
-        resident_kernel, (rows_of,) * 3, decode_q, cache_k, cache_v, cache_len.reshape(1, REQ)
-    )
-    asked, prefill_out, columns, home = lax.optimization_barrier(
-        (asked, prefill_out, columns, home)
-    )
+        resident_kernel, (rows_of,) * 3, decode_q, cache_k, cache_v, cache_len.reshape(1, REQ), flops=shadow_flops
+    )
+    asked, other, home = lax.optimization_barrier((asked, other, home))
     sent = call(
         page_kernel,
-        jax.ShapeDtypeStruct((groups, CAP, width + HD), bf16),
+        jax.ShapeDtypeStruct((peers, 2 * CAP, width + HD), bf16),
+        core,
         asked,
-        key_rot,
-        prefill_v,
-        owner,
-        slot_index,
-        (page_request + 1)[:, None],
-    )
-    got = lax.all_to_all(sent, grp, split_axis=0, concat_axis=0, tiled=True)
-    got = got.reshape(groups * CAP, width + HD)
-
-    peers = lax.axis_size(("y", "x"))
+        own,
+        other,
+        scalars=1,
+    )
+    got = lax.all_to_all(sent, chips, split_axis=0, concat_axis=0, tiled=True)
+    got = got.reshape(peers * 2 * CAP, width + HD)
+
     repeated = call(
         combine_kernel, jax.ShapeDtypeStruct((peers, REQ, width), bf16), got, *home
     )
-    everyone = lax.all_to_all(repeated, ("y", "x"), split_axis=0, concat_axis=0, tiled=True)
+    everyone = lax.all_to_all(repeated, chips, split_axis=0, concat_axis=0, tiled=True)
     everyone = everyone.reshape(peers * REQ, width)
     shards = lax.axis_size("z")
     cores = lax.axis_size("c")
-    terms = jnp.einsum("ad,cde->cae", everyone, columns, preferred_element_type=f32).astype(bf16)
+    terms = call(
+        project_kernel,
+        jax.ShapeDtypeStruct((cores, peers * REQ, HD), bf16),
+        core,
+        everyone,
+        own,
+        other,
+        scalars=1,
+    )
     terms = terms.reshape(cores * shards, peers * REQ // shards, HD)
+    prefill_out = call(
+        prefill_kernel,
+        jax.ShapeDtypeStruct(prefill_q.shape, bf16),
+        prefill_q,
+        own,
+        cosine,
+        sine_part,
+        terms,
+        unread=1,
+        flops=shadow_flops,
+    )
     terms = lax.all_to_all(terms, ("c", "z"), split_axis=0, concat_axis=0, tiled=True)
     decode_out = call(
         sum_kernel, jax.ShapeDtypeStruct((peers * REQ * cores // shards, HD), bf16), terms

time: 78.2 us -> 76.2 us (0.974)
  blocking collectives: 48.1 us -> 30.5 us
  starting transfers between devices: 14.1 us -> 26.4 us
  waiting for transfers between devices: 5.18 us -> 7.39 us
    all_to_all x3 -> x2, blocking collectives: 48.1 us -> 30.5 us  [the longest x1 17.4 us: on_device(): got = lax.all_to_all(sent, chips, split_axis=0, concat_axis=0, tiled=True)]
    all_to_all x1 -> x2, starting transfers between devices: 11.8 us -> 23.5 us  [the longest x1 13 us: on_device(): lax.all_to_all(terms, ('c', 'z'), split_axis=0, concat_axis=0, tiled=True)]
    all_to_all x1 -> x2, waiting for transfers between devices: 5.17 us -> 7.39 us  [the longest x1 5.29 us: on_device(): lax.all_to_all(terms, ('c', 'z'), split_axis=0, concat_axis=0, tiled=True)]
    unnamed x22, local copies, waits for them, and re-layouts: 2.02 us -> 3.09 us
    pallas_call x6 -> x8, Pallas kernels: 5.58 us -> 6.26 us  [call(): pl.pallas_call(kernel, out_shape=outs, in_specs=[pl.BlockSpec(memory_spac...]
  transfers between devices with their start and end apart: 2 -> 3, of which waited for: 1 -> 2; matrix products, arithmetic and copies ran while one was open for 1% -> 1% of each run, Pallas kernels for 3% -> 3%
where the time goes in v4:
time: 76.2 us; the launch traced here: 75.7 us
  blocking collectives  30.5 us (40%)
  starting transfers between devices  26.4 us (35%)
  waiting for transfers between devices  7.39 us (10%)
  Pallas kernels  6.26 us (8%)
  local copies, waits for them, and re-layouts  3.2 us (4%)
  between operations  1.45 us (2%)
    all_to_all x1, blocking collectives, on_device(): got = lax.all_to_all(sent, chips, split_axis=0, concat_axis=0, tiled=True)  17.4 us
    all_to_all x1, blocking collectives, on_device(): lax.all_to_all(repeated, chips, split_axis=0, concat_axis=0, tiled=True)  13.1 us
    all_to_all x1, starting transfers between devices, on_device(): lax.all_to_all(terms, ('c', 'z'), split_axis=0, concat_axis=0, tiled=True)  13 us
    all_to_all x1, starting transfers between devices, on_device(): lax.all_to_all(asking, chips, split_axis=0, concat_axis=0, tiled=True)  10.5 us
    pallas_call x8, Pallas kernels, call(): pl.pallas_call(kernel, out_shape=outs, in_specs=[pl.BlockSpec(memory_spac...  6.26 us
    all_to_all x1, waiting for transfers between devices, on_device(): lax.all_to_all(terms, ('c', 'z'), split_axis=0, concat_axis=0, tiled=True)  5.29 us
    unnamed x22, local copies, waits for them, and re-layouts  3.09 us
    ppermute x1, starting transfers between devices, on_device(): other = lax.ppermute(own, 'c', [(0, 1), (1, 0)])  2.86 us
  transfers between devices with their start and end apart: 3, of which 2 were waited for; matrix products, arithmetic and copies ran while one was open for 1% of the time, Pallas kernels for 3%

profile of v4, /device:TPU:1, one launch (start us, length us, event | category | flops | bytes accessed | tf_op | source)
XLA Modules:
  0.0 75.7 jit_solution(15456184091441489962)
XLA Ops:
  0.6 0.0 copy-start.3
  0.6 0.7 copy-done.3
  1.3 0.7 shard_map.122._
  2.0 10.5 %all-to-all-start = ((bf16[32,4,512]{2,1,0:T(4,128)(2,1)}), bf16[32,4,512]{2,1,0:T(4,128)(2,1)S(1)}, u32[]{:S(2)}, u32[]{:S(2)}) async-start(bf16[32,4,512]{2,1,0:T(4,128)(2,1)} %shard_map.122._), calls=%async_computation | async-start | bytes 262144 | tf_op jit(solution)/shard_map/all_to_all | solution.py:240
  13.2 0.0 copy-start
  13.2 0.0 copy-start.1
  13.2 0.0 copy-start.2
  13.2 0.5 fusion
  13.7 0.0 copy-start.5
  13.8 0.0 copy-start.6
  13.8 0.0 copy-start.7
  13.8 0.3 copy-done
  14.1 0.0 copy-done.1
  14.1 0.0 copy-done.2
  14.1 0.3 copy-done.5
  14.4 0.0 copy-done.6
  14.5 0.2 shard_map.123.own_ref.pack_ref
  14.6 2.9 %collective-permute-start = (bf16[1040,128]{1,0:T(8,128)(2,1)S(1)}, bf16[1040,128]{1,0:T(8,128)(2,1)S(1)}, u32[]{:S(2)}, u32[]{:S(2)}) collective-permute-start(bf16[1040,128]{1,0:T(8,128)(2,1)S(1)} %shard_map.123.own_ref.pack_ref), channel_id=1, source_target_pairs={{0,8},{8,0},{1,9},{9,1},{2,10},{10,2},{3,11},{11,3},{4,12},{12,4},... | collective-permute-start | bytes 798728 | tf_op jit(solution)/shard_map/ppermute | solution.py:258
  17.5 0.0 copy-start.4
  17.5 0.0 copy-start.10
  17.5 0.0 copy-done.7
  17.5 0.7 copy-done.4
  18.2 0.0 copy-done.10
  18.2 0.0 copy-start.8
  18.2 1.0 %copy-done.8 = bf16[4,512,128]{2,1,0:T(8,128)(2,1)S(1)} copy-done((bf16[4,512,128]{2,1,0:T(8,128)(2,1)S(1)}, bf16[4,512,128]{2,1,0:T(8,128)(2,1)}, u32[]{:S(2)}) %copy-start.8) | copy-done | bytes 524312
  19.2 0.5 shard_map.124
  19.7 2.1 %all-to-all-done = bf16[32,4,512]{2,1,0:T(4,128)(2,1)S(1)} async-done(((bf16[32,4,512]{2,1,0:T(4,128)(2,1)}), bf16[32,4,512]{2,1,0:T(4,128)(2,1)S(1)}, u32[]{:S(2)}, u32[]{:S(2)}) %all-to-all-start) | async-done | bytes 131104 | tf_op jit(solution)/shard_map/all_to_all | solution.py:240
  21.9 0.0 collective-permute-done.other_ref
  21.9 1.2 %shard_map.125 = bf16[32,4,640]{2,1,0:T(4,128)(2,1)S(1)} custom-call(s32[1]{0:T(128)} %bitcast.3.core_ref, bf16[128,512]{1,0:T(8,128)(2,1)S(1)} %reshape.53.q_ref, bf16[1040,128]{1,0:T(8,128)(2,1)S(1)} %shard_map.123.own_ref.pack_ref, bf16[1040,128]{1,0:T(8,128)(2,1)S(1)} %collective-permute-done.other_ref), custom_call_target="tpu_custom_call" | custom-call | bytes 827396 | tf_op jit(solution)/shard_map/pallas_call | solution.py:49
  23.1 17.4 %all_to_all.20 = bf16[32,4,640]{2,1,0:T(4,128)(2,1)S(1)} all-to-all(bf16[32,4,640]{2,1,0:T(4,128)(2,1)S(1)} %shard_map.125), channel_id=1, replica_groups=mesh['y'=8,'x'=4,'c'=2,'z'=8] {'y','x'}, dimensions={0} | all-to-all | bytes 327680 | tf_op jit(solution)/shard_map/all_to_all | solution.py:274
  40.6 0.3 shard_map.126
  40.9 13.1 %all_to_all.21 = bf16[32,4,512]{2,1,0:T(4,128)(2,1)S(1)} all-to-all(bf16[32,4,512]{2,1,0:T(4,128)(2,1)S(1)} %shard_map.126), channel_id=1, replica_groups=mesh['y'=8,'x'=4,'c'=2,'z'=8] {'y','x'}, dimensions={0} | all-to-all | bytes 262144 | tf_op jit(solution)/shard_map/all_to_all | solution.py:280
  54.0 0.0 copy-start.9
  54.1 0.9 %shard_map.127 = bf16[2,128,128]{2,1,0:T(8,128)(2,1)} custom-call(s32[1]{0:T(128)} %bitcast.3.core_ref, bf16[128,512]{1,0:T(8,128)(2,1)S(1)} %reshape.56.rows_ref, bf16[1040,128]{1,0:T(8,128)(2,1)S(1)} %shard_map.123.own_ref.pack_ref, bf16[1040,128]{1,0:T(8,128)(2,1)S(1)} %collective-permute-done.other_ref), custom_call_target="tpu_custom_call" | custom-call | bytes 729092 | tf_op jit(solution)/shard_map/pallas_call | solution.py:49
  54.9 13.0 %all-to-all-start.3 = ((bf16[16,16,128]{2,1,0:T(8,128)(2,1)}), bf16[16,16,128]{2,1,0:T(8,128)(2,1)S(1)}, u32[]{:S(2)}, u32[]{:S(2)}) async-start(bf16[16,16,128]{2,1,0:T(8,128)(2,1)} %bitcast.5._), calls=%async_computation.3 | async-start | bytes 131072 | tf_op jit(solution)/shard_map/all_to_all | solution.py:305
  67.9 0.0 copy-done.9
  67.9 1.9 %shard_map.128 = bf16[256,512]{1,0:T(8,128)(2,1)} custom-call(bf16[256,512]{1,0:T(8,128)(2,1)S(1)} %copy-done.9, bf16[1040,128]{1,0:T(8,128)(2,1)S(1)} %shard_map.123.own_ref.pack_ref, f32[256,128]{1,0:T(8,128)S(1)} %get-tuple-element.19.cos_ref, f32[256,128]{1,0:T(8,128)S(1)} %get-tuple-element.18.sin_ref, bf16[16,16,128]{2,1,0:T(8,128)(2,1)} %bitcast.5._), custom_call_target="tpu_custom_call" | custom-call | flops 5000000000 | bytes 1118208 | tf_op jit(solution)/shard_map/pallas_call | solution.py:49
  69.8 5.3 %all-to-all-done.3.terms_ref = bf16[16,16,128]{2,1,0:T(8,128)(2,1)S(1)} async-done(((bf16[16,16,128]{2,1,0:T(8,128)(2,1)}), bf16[16,16,128]{2,1,0:T(8,128)(2,1)S(1)}, u32[]{:S(2)}, u32[]{:S(2)}) %all-to-all-start.3) | async-done | bytes 65568 | tf_op jit(solution)/shard_map/all_to_all | solution.py:305
  75.1 0.6 shard_map.129
  (5 shorter events, 0.1 us)
Async XLA Ops:
  0.6 0.7 copy-start.3
  2.0 19.9 %all-to-all-start = ((bf16[32,4,512]{2,1,0:T(4,128)(2,1)}), bf16[32,4,512]{2,1,0:T(4,128)(2,1)S(1)}, u32[]{:S(2)}, u32[]{:S(2)}) async-start(bf16[32,4,512]{2,1,0:T(4,128)(2,1)} %shard_map.122._), calls=%async_computation | async-start | bytes 262144 | tf_op jit(solution)/shard_map/all_to_all | solution.py:240
  13.2 0.9 %copy-start = (bf16[512,128]{1,0:T(8,128)(2,1)S(1)}, bf16[512,128]{1,0:T(8,128)(2,1)}, u32[]{:S(2)}) copy-start(bf16[512,128]{1,0:T(8,128)(2,1)} %weight_ref.1) | copy-start | bytes 393220
  13.2 0.9 %copy-start.1 = (bf16[256,128]{1,0:T(8,128)(2,1)S(1)}, bf16[256,128]{1,0:T(8,128)(2,1)}, u32[]{:S(2)}) copy-start(bf16[256,128]{1,0:T(8,128)(2,1)} %k_ref.2) | copy-start | bytes 196612
  13.2 0.9 %copy-start.2 = (bf16[256,128]{1,0:T(8,128)(2,1)S(1)}, bf16[256,128]{1,0:T(8,128)(2,1)}, u32[]{:S(2)}) copy-start(bf16[256,128]{1,0:T(8,128)(2,1)} %v_ref.2) | copy-start | bytes 196612
  13.7 0.7 copy-start.5
  13.8 0.7 copy-start.6
  13.8 3.7 %copy-start.7 = (bf16[4,512,128]{2,1,0:T(8,128)(2,1)S(1)}, bf16[4,512,128]{2,1,0:T(8,128)(2,1)}, u32[]{:S(2)}) copy-start(bf16[4,512,128]{2,1,0:T(8,128)(2,1)} %k_ref.3) | copy-start | bytes 1572868
  14.6 7.3 %collective-permute-start = (bf16[1040,128]{1,0:T(8,128)(2,1)S(1)}, bf16[1040,128]{1,0:T(8,128)(2,1)S(1)}, u32[]{:S(2)}, u32[]{:S(2)}) collective-permute-start(bf16[1040,128]{1,0:T(8,128)(2,1)S(1)} %shard_map.123.own_ref.pack_ref), channel_id=1, source_target_pairs={{0,8},{8,0},{1,9},{9,1},{2,10},{10,2},{3,11},{11,3},{4,12},{12,4},... | collective-permute-start | bytes 798728 | tf_op jit(solution)/shard_map/ppermute | solution.py:258
  17.5 0.7 copy-start.4
  17.5 0.7 copy-start.10
  18.2 1.0 %copy-start.8 = (bf16[4,512,128]{2,1,0:T(8,128)(2,1)S(1)}, bf16[4,512,128]{2,1,0:T(8,128)(2,1)}, u32[]{:S(2)}) copy-start(bf16[4,512,128]{2,1,0:T(8,128)(2,1)} %v_ref.3) | copy-start | bytes 1572868
  54.0 13.9 %copy-start.9 = (bf16[256,512]{1,0:T(8,128)(2,1)S(1)}, bf16[256,512]{1,0:T(8,128)(2,1)}, u32[]{:S(2)}) copy-start(bf16[256,512]{1,0:T(8,128)(2,1)} %q_ref.5) | copy-start | bytes 786436
  54.9 20.2 %all-to-all-start.3 = ((bf16[16,16,128]{2,1,0:T(8,128)(2,1)}), bf16[16,16,128]{2,1,0:T(8,128)(2,1)S(1)}, u32[]{:S(2)}, u32[]{:S(2)}) async-start(bf16[16,16,128]{2,1,0:T(8,128)(2,1)} %bitcast.5._), calls=%async_computation.3 | async-start | bytes 131072 | tf_op jit(solution)/shard_map/all_to_all | solution.py:305

commit v5 on v4

--- a/solution.py
+++ b/solution.py
@@ -22,16 +22,28 @@
 vmem_limit = 32 * 1024 * 1024
 shadow_flops = 5 * 10**9
 CH = 256
+at_requests, at_lengths, at_offset, at_core = 16, 32, 32 + REQ, 33 + REQ
 at_values, at_info, at_weight, at_end = CH, 2 * CH, 2 * CH + 16, 2 * CH + 16 + 512
 
 
-def angles(offset, row_count):
-    lane = jnp.arange(HD, dtype=jnp.int32)
-    frequency = rope_base ** (-2.0 * (lane % (HD // 2)).astype(f32) / HD)
-    positions = offset + jnp.arange(row_count, dtype=jnp.int32)
-    angle_rad = positions.astype(f32)[:, None] * frequency[None, :]
+def factors(offset):
+    shape = (16, HD)
+    lane, row = iota(shape, 1), iota(shape, 0)
+    power = (lane % (HD // 2)).astype(f32) * (-2.0 / HD * math.log(rope_base))
+    frequency = jnp.exp(power)
     sign = jnp.where(lane < HD // 2, -1.0, 1.0)
-    return jnp.cos(angle_rad), jnp.sin(angle_rad) * sign[None, :]
+
+    def turn(position):
+        angle_rad = position.astype(f32) * frequency
+        return jnp.cos(angle_rad), jnp.sin(angle_rad) * sign
+
+    fine, coarse = turn(row), turn(offset + 16 * row)
+    cosine, sine_part = [], []
+    for d in range(CH // 16):
+        c, s = coarse[0][d : d + 1], coarse[1][d : d + 1]
+        cosine.append(fine[0] * c - fine[1] * s)
+        sine_part.append(fine[1] * c + fine[0] * s)
+    return jnp.concatenate(cosine, axis=0), jnp.concatenate(sine_part, axis=0)
 
 
 def dot(a, b, dims):
@@ -42,10 +54,9 @@
     return lax.broadcasted_iota(jnp.int32, shape, axis)
 
 
-def call(kernel, outs, *args, scalars=0, unread=0, flops=0):
+def call(kernel, outs, *args, unread=0, flops=0):
     moved = sum(a.size * a.dtype.itemsize for a in (*args, *jax.tree.leaves(outs)))
-    places = [pltpu.SMEM] * scalars + [pltpu.VMEM] * (len(args) - scalars - unread)
-    places += [pl.ANY] * unread
+    places = [pltpu.VMEM] * (len(args) - unread) + [pl.ANY] * unread
     return pl.pallas_call(
         kernel,
         out_shape=outs,
@@ -61,27 +72,29 @@
 
 
 def pack_kernel(
-    k_ref, v_ref, cos_ref, sin_ref, group_ref, request_ref, weight_ref, _, pack_ref
+    ints_ref, k_ref, v_ref, weight_ref, _, pack_ref
 ):
-    pack_ref[:at_values, :] = rotate(k_ref[...], cos_ref[...], sin_ref[...])
+    pack_ref[:at_values, :] = rotate(k_ref[...], *factors(ints_ref[:, at_offset : at_offset + 1]))
     pack_ref[at_values:at_info, :] = v_ref[...]
     pack_ref[at_weight:, :] = weight_ref[...]
 
-    pages = group_ref.shape[1]
+    pages = at_requests
     eye = iota((pages, pages), 0) == iota((pages, pages), 1)
-    group_row = group_ref[...].astype(f32)
+    group_row = ints_ref[:, :pages].astype(f32)
     group = jnp.sum(jnp.where(eye, group_row, 0.0), axis=1, keepdims=True)
-    request = jnp.sum(jnp.where(eye, request_ref[...].astype(f32), 0.0), axis=1, keepdims=True)
+    request = jnp.sum(jnp.where(eye, ints_ref[:, at_requests:at_lengths].astype(f32), 0.0), axis=1, keepdims=True)
     before = iota((pages, pages), 1) < iota((pages, pages), 0)
     earlier = jnp.where(before & (group == group_row), 1.0, 0.0)
     earlier = jnp.sum(earlier, axis=1, keepdims=True)
     lane = iota((pages, HD), 1)
+    core = ints_ref[:, at_core : at_core + 1].astype(f32)
     info = jnp.where(lane == 0, group, jnp.where(lane == 1, request, earlier))
+    info = jnp.where(lane == 3, core, info)
     pack_ref[at_info:at_weight, :] = info.astype(bf16)
 
 
-def prefill_kernel(q_ref, pack_ref, cos_ref, sin_ref, _, out_ref):
-    cosine, sine_part = cos_ref[...], sin_ref[...]
+def prefill_kernel(ints_ref, q_ref, pack_ref, _, out_ref):
+    cosine, sine_part = factors(ints_ref[:, at_offset : at_offset + 1])
     keys, values = pack_ref[:at_values, :], pack_ref[at_values:at_info, :]
     causal = iota((CH, CH), 1) <= iota((CH, CH), 0)
     for h in range(QPK):
@@ -94,15 +107,14 @@
         out_ref[:, part] = dot(weights.astype(bf16), values, ((1,), (0,))).astype(bf16)
 
 
-def resident_kernel(q_ref, k_ref, v_ref, len_ref, sum_ref, peak_ref, total_ref):
-    q = q_ref[...].astype(f32)
-    rows = jnp.concatenate([q[:, h * HD : (h + 1) * HD] for h in range(QPK)], axis=0).astype(bf16)
+def resident_kernel(rows_ref, k_ref, v_ref, ints_ref, sum_ref, peak_ref, total_ref):
+    rows = rows_ref[...]
     slots = k_ref.shape[1]
     request = iota((ROWS, 1), 0) % REQ
     live = jnp.zeros((ROWS, 1), jnp.int32)
     scores = jnp.zeros((ROWS, slots), f32)
     for r in range(REQ):
-        live = jnp.where(request == r, len_ref[:, r : r + 1], live)
+        live = jnp.where(request == r, ints_ref[:, at_lengths + r : at_lengths + r + 1], live)
         scores = jnp.where(request == r, dot(rows, k_ref[r], ((1,), (1,))), scores)
     shown = iota((ROWS, slots), 1) < live
     scores = jnp.where(shown, scores * scale, neg_large)
@@ -118,8 +130,11 @@
     total_ref[...] = jnp.broadcast_to(total, (ROWS, HD))
 
 
-def repeat_kernel(q_ref, out_ref):
+def repeat_kernel(q_ref, out_ref, rows_ref):
     out_ref[...] = jnp.broadcast_to(q_ref[...][None], out_ref.shape)
+    q = q_ref[...].astype(f32)
+    rows = jnp.concatenate([q[:, h * HD : (h + 1) * HD] for h in range(QPK)], axis=0)
+    rows_ref[...] = rows.astype(bf16)
 
 
 def parts_of(value, count):
@@ -131,8 +146,8 @@
     return parts
 
 
-def page_kernel(core_ref, q_ref, own_ref, other_ref, out_ref):
-    core = core_ref[0].astype(f32)
+def page_kernel(q_ref, own_ref, other_ref, out_ref):
+    core = own_ref[at_info:at_weight, :].astype(f32)[:, 3:4]
     pages = at_weight - at_info
     slots = out_ref.shape[0] * out_ref.shape[1]
     placed = jnp.zeros((slots, out_ref.shape[2]), f32)
@@ -171,11 +186,13 @@
     out_ref[...] = placed.reshape(out_ref.shape).astype(bf16)
 
 
-def project_kernel(core_ref, rows_ref, own_ref, other_ref, out_ref):
-    core = core_ref[0]
-    for index, ref in ((core, own_ref), (1 - core, other_ref)):
-        product = dot(rows_ref[...], ref[at_weight:, :], ((1,), (0,)))
-        out_ref[index] = product.astype(bf16)
+def project_kernel(rows_ref, own_ref, other_ref, out_ref):
+    first = own_ref[at_info : at_info + 16, :].astype(f32)[0:1, 3:4] == 0.0
+    rows = rows_ref[...]
+    own = dot(rows, own_ref[at_weight:, :], ((1,), (0,)))
+    other = dot(rows, other_ref[at_weight:, :], ((1,), (0,)))
+    out_ref[0] = jnp.where(first, own, other).astype(bf16)
+    out_ref[1] = jnp.where(first, other, own).astype(bf16)
 
 
 def combine_kernel(got_ref, sum_ref, peak_ref, total_ref, out_ref):
@@ -236,21 +253,28 @@
     peers = lax.axis_size(chips)
     width = decode_q.shape[1]
 
-    asking = call(repeat_kernel, jax.ShapeDtypeStruct((peers,) + decode_q.shape, bf16), decode_q)
+    asking, rows = call(
+        repeat_kernel,
+        (
+            jax.ShapeDtypeStruct((peers,) + decode_q.shape, bf16),
+            jax.ShapeDtypeStruct((ROWS, HD), bf16),
+        ),
+        decode_q,
+    )
     asked = lax.all_to_all(asking, chips, split_axis=0, concat_axis=0, tiled=True)
     asked = asked.reshape(peers * REQ, width)
 
     core = lax.axis_index("c").reshape(1)
-    cosine, sine_part = angles(span_offset[0], prefill_q.shape[0])
+    small, ints = (page_group[:, 0], page_request, cache_len, span_offset, core), 0
+    for piece, start in zip(small, (0, at_requests, at_lengths, at_offset, at_core)):
+        ints = ints + jnp.pad(piece, (start, HD - start - piece.shape[0]))
+    ints = ints.reshape(1, HD)
     own = call(
         pack_kernel,
         jax.ShapeDtypeStruct((at_end, HD), bf16),
+        ints,
         prefill_k,
         prefill_v,
-        cosine,
-        sine_part,
-        page_group.reshape(1, -1),
-        page_request.reshape(1, -1),
         out_weight,
         asking,
         unread=1,
@@ -259,17 +283,21 @@
 
     rows_of = jax.ShapeDtypeStruct((ROWS, HD), f32)
     home = call(
-        resident_kernel, (rows_of,) * 3, decode_q, cache_k, cache_v, cache_len.reshape(1, REQ), flops=shadow_flops
+        resident_kernel,
+        (rows_of,) * 3,
+        rows,
+        cache_k,
+        cache_v,
+        ints,
+        flops=shadow_flops,
     )
     asked, other, home = lax.optimization_barrier((asked, other, home))
     sent = call(
         page_kernel,
         jax.ShapeDtypeStruct((peers, 2 * CAP, width + HD), bf16),
-        core,
         asked,
         own,
         other,
-        scalars=1,
     )
     got = lax.all_to_all(sent, chips, split_axis=0, concat_axis=0, tiled=True)
     got = got.reshape(peers * 2 * CAP, width + HD)
@@ -284,20 +312,17 @@
     terms = call(
         project_kernel,
         jax.ShapeDtypeStruct((cores, peers * REQ, HD), bf16),
-        core,
         everyone,
         own,
         other,
-        scalars=1,
     )
     terms = terms.reshape(cores * shards, peers * REQ // shards, HD)
     prefill_out = call(
         prefill_kernel,
         jax.ShapeDtypeStruct(prefill_q.shape, bf16),
+        ints,
         prefill_q,
         own,
-        cosine,
-        sine_part,
         terms,
         unread=1,
         flops=shadow_flops,

time: 76.2 us -> 74.4 us (0.976)
  blocking collectives: 30.5 us -> 28.6 us
  waiting for transfers between devices: 7.39 us -> 9.17 us
  local copies, waits for them, and re-layouts: 3.2 us -> 1.86 us
    all_to_all x1, waiting for transfers between devices: 2.09 us -> 3.94 us  [on_device(): lax.all_to_all(asking, chips, split_axis=0, concat_axis=0, tiled=True)]
    all_to_all x1, blocking collectives: 17.4 us -> 15.6 us  [on_device(): got = lax.all_to_all(sent, chips, split_axis=0, concat_axis=0, tiled=True)]
    unnamed x22 -> x20, local copies, waits for them, and re-layouts: 3.09 us -> 1.75 us
  transfers between devices with their start and end apart: 3 -> 3, of which waited for: 2 -> 2; matrix products, arithmetic and copies ran while one was open for 1% -> 0% of each run, Pallas kernels for 3% -> 4%
where the time goes in v5:
time: 74.4 us; the launch traced here: 74 us
  blocking collectives  28.6 us (38%)
  starting transfers between devices  26.5 us (36%)
  waiting for transfers between devices  9.17 us (12%)
  Pallas kernels  6.32 us (8%)
  local copies, waits for them, and re-layouts  1.86 us (2%)
  between operations  1.41 us (2%)
    all_to_all x1, blocking collectives, on_device(): got = lax.all_to_all(sent, chips, split_axis=0, concat_axis=0, tiled=True)  15.6 us
    all_to_all x1, blocking collectives, on_device(): lax.all_to_all(repeated, chips, split_axis=0, concat_axis=0, tiled=True)  13.1 us
    all_to_all x1, starting transfers between devices, on_device(): lax.all_to_all(terms, ('c', 'z'), split_axis=0, concat_axis=0, tiled=True)  13 us
    all_to_all x1, starting transfers between devices, on_device(): lax.all_to_all(asking, chips, split_axis=0, concat_axis=0, tiled=True)  10.6 us
    pallas_call x8, Pallas kernels, call(): pl.pallas_call(kernel, out_shape=outs, in_specs=[pl.BlockSpec(memory_spac...  6.32 us
    all_to_all x1, waiting for transfers between devices, on_device(): lax.all_to_all(terms, ('c', 'z'), split_axis=0, concat_axis=0, tiled=True)  5.22 us
    all_to_all x1, waiting for transfers between devices, on_device(): lax.all_to_all(asking, chips, split_axis=0, concat_axis=0, tiled=True)  3.94 us
    ppermute x1, starting transfers between devices, on_device(): other = lax.ppermute(own, 'c', [(0, 1), (1, 0)])  2.86 us
  transfers between devices with their start and end apart: 3, of which 2 were waited for; matrix products, arithmetic and copies ran while one was open for 0% of the time, Pallas kernels for 4%

profile of v5, /device:TPU:1, one launch (start us, length us, event | category | flops | bytes accessed | tf_op | source)
XLA Modules:
  0.0 74.0 jit_solution(1664786375449684162)
XLA Ops:
  0.6 0.0 copy-start.3
  0.6 0.7 copy-done.3
  1.3 0.0 copy-start.7
  1.3 0.0 copy-start.8
  1.3 0.0 copy-start.9
  1.3 0.7 shard_map.122
  2.0 0.0 copy-start
  2.0 0.0 copy-start.1
  2.0 0.0 copy-start.2
  2.0 0.0 copy-start.4
  2.0 10.6 %all-to-all-start = ((bf16[32,4,512]{2,1,0:T(4,128)(2,1)}), bf16[32,4,512]{2,1,0:T(4,128)(2,1)S(1)}, u32[]{:S(2)}, u32[]{:S(2)}) async-start(bf16[32,4,512]{2,1,0:T(4,128)(2,1)} %get-tuple-element.12._), calls=%async_computation | async-start | bytes 262144 | tf_op jit(solution)/shard_map/all_to_all | solution.py:264
  13.3 0.0 copy-done.7
  13.3 0.0 copy-done.8
  13.3 0.0 copy-done.9
  13.3 0.1 add_bitcast_fusion.ints_ref
  13.4 0.0 copy-done
  13.4 0.0 copy-done.1
  13.4 0.0 copy-done.2
  13.4 0.2 shard_map.123.own_ref.pack_ref
  13.6 2.9 %collective-permute-start = (bf16[1040,128]{1,0:T(8,128)(2,1)S(1)}, bf16[1040,128]{1,0:T(8,128)(2,1)S(1)}, u32[]{:S(2)}, u32[]{:S(2)}) collective-permute-start(bf16[1040,128]{1,0:T(8,128)(2,1)S(1)} %shard_map.123.own_ref.pack_ref), channel_id=1, source_target_pairs={{0,8},{8,0},{1,9},{9,1},{2,10},{10,2},{3,11},{11,3},{4,12},{12,4},... | collective-permute-start | bytes 798728 | tf_op jit(solution)/shard_map/ppermute | solution.py:282
  16.5 0.0 copy-done.4
  16.5 0.0 copy-start.5
  16.5 1.0 %copy-done.5 = bf16[4,512,128]{2,1,0:T(8,128)(2,1)S(1)} copy-done((bf16[4,512,128]{2,1,0:T(8,128)(2,1)S(1)}, bf16[4,512,128]{2,1,0:T(8,128)(2,1)}, u32[]{:S(2)}) %copy-start.5) | copy-done | bytes 524312
  17.5 0.5 shard_map.124
  18.1 3.9 %all-to-all-done = bf16[32,4,512]{2,1,0:T(4,128)(2,1)S(1)} async-done(((bf16[32,4,512]{2,1,0:T(4,128)(2,1)}), bf16[32,4,512]{2,1,0:T(4,128)(2,1)S(1)}, u32[]{:S(2)}, u32[]{:S(2)}) %all-to-all-start) | async-done | bytes 131104 | tf_op jit(solution)/shard_map/all_to_all | solution.py:264
  22.0 0.0 collective-permute-done.other_ref
  22.0 1.2 %shard_map.125 = bf16[32,4,640]{2,1,0:T(4,128)(2,1)S(1)} custom-call(bf16[128,512]{1,0:T(8,128)(2,1)S(1)} %reshape.24.q_ref, bf16[1040,128]{1,0:T(8,128)(2,1)S(1)} %shard_map.123.own_ref.pack_ref, bf16[1040,128]{1,0:T(8,128)(2,1)S(1)} %collective-permute-done.other_ref), custom_call_target="tpu_custom_call" | custom-call | bytes 827392 | tf_op jit(solution)/shard_map/pallas_call | solution.py:60
  23.3 15.6 %all_to_all.20 = bf16[32,4,640]{2,1,0:T(4,128)(2,1)S(1)} all-to-all(bf16[32,4,640]{2,1,0:T(4,128)(2,1)S(1)} %shard_map.125), channel_id=1, replica_groups=mesh['y'=8,'x'=4,'c'=2,'z'=8] {'y','x'}, dimensions={0} | all-to-all | bytes 327680 | tf_op jit(solution)/shard_map/all_to_all | solution.py:302
  38.9 0.3 shard_map.126
  39.2 13.1 %all_to_all.21 = bf16[32,4,512]{2,1,0:T(4,128)(2,1)S(1)} all-to-all(bf16[32,4,512]{2,1,0:T(4,128)(2,1)S(1)} %shard_map.126), channel_id=1, replica_groups=mesh['y'=8,'x'=4,'c'=2,'z'=8] {'y','x'}, dimensions={0} | all-to-all | bytes 262144 | tf_op jit(solution)/shard_map/all_to_all | solution.py:308
  52.4 0.0 copy-start.6
  52.4 0.8 %shard_map.127 = bf16[2,128,128]{2,1,0:T(8,128)(2,1)} custom-call(bf16[128,512]{1,0:T(8,128)(2,1)S(1)} %reshape.26.rows_ref, bf16[1040,128]{1,0:T(8,128)(2,1)S(1)} %shard_map.123.own_ref.pack_ref, bf16[1040,128]{1,0:T(8,128)(2,1)S(1)} %collective-permute-done.other_ref), custom_call_target="tpu_custom_call" | custom-call | bytes 729088 | tf_op jit(solution)/shard_map/pallas_call | solution.py:60
  53.2 13.0 %all-to-all-start.3 = ((bf16[16,16,128]{2,1,0:T(8,128)(2,1)}), bf16[16,16,128]{2,1,0:T(8,128)(2,1)S(1)}, u32[]{:S(2)}, u32[]{:S(2)}) async-start(bf16[16,16,128]{2,1,0:T(8,128)(2,1)} %bitcast.3._), calls=%async_computation.3 | async-start | bytes 131072 | tf_op jit(solution)/shard_map/all_to_all | solution.py:330
  66.2 0.0 copy-done.6
  66.2 1.9 %shard_map.128 = bf16[256,512]{1,0:T(8,128)(2,1)} custom-call(s32[1,128]{1,0:T(1,128)S(1)} %add_bitcast_fusion.ints_ref, bf16[256,512]{1,0:T(8,128)(2,1)S(1)} %copy-done.6, bf16[1040,128]{1,0:T(8,128)(2,1)S(1)} %shard_map.123.own_ref.pack_ref, bf16[16,16,128]{2,1,0:T(8,128)(2,1)} %bitcast.3._), custom_call_target="tpu_custom_call" | custom-call | flops 5000000000 | bytes 856576 | tf_op jit(solution)/shard_map/pallas_call | solution.py:60
  68.2 5.2 %all-to-all-done.3.terms_ref = bf16[16,16,128]{2,1,0:T(8,128)(2,1)S(1)} async-done(((bf16[16,16,128]{2,1,0:T(8,128)(2,1)}), bf16[16,16,128]{2,1,0:T(8,128)(2,1)S(1)}, u32[]{:S(2)}, u32[]{:S(2)}) %all-to-all-start.3) | async-done | bytes 65568 | tf_op jit(solution)/shard_map/all_to_all | solution.py:330
  73.4 0.6 shard_map.129
  (3 shorter events, 0.1 us)
Async XLA Ops:
  0.6 0.7 copy-start.3
  1.3 12.0 %copy-start.7 = (s32[4]{0:T(128)S(1)}, s32[4]{0:T(128)}, u32[]{:S(2)}) copy-start(s32[4]{0:T(128)} %param.20) | copy-start | bytes 52
  1.3 12.0 %copy-start.8 = (s32[16]{0:T(128)S(1)}, s32[16]{0:T(128)}, u32[]{:S(2)}) copy-start(s32[16]{0:T(128)} %param.16) | copy-start | bytes 196
  1.3 12.0 %copy-start.9 = (s32[16,1]{0,1:T(1,128)S(1)}, s32[16,1]{0,1:T(1,128)}, u32[]{:S(2)}) copy-start(s32[16,1]{0,1:T(1,128)} %param.15) | copy-start | bytes 196
  2.0 11.4 %copy-start = (bf16[512,128]{1,0:T(8,128)(2,1)S(1)}, bf16[512,128]{1,0:T(8,128)(2,1)}, u32[]{:S(2)}) copy-start(bf16[512,128]{1,0:T(8,128)(2,1)} %weight_ref.1) | copy-start | bytes 393220
  2.0 11.4 %copy-start.1 = (bf16[256,128]{1,0:T(8,128)(2,1)S(1)}, bf16[256,128]{1,0:T(8,128)(2,1)}, u32[]{:S(2)}) copy-start(bf16[256,128]{1,0:T(8,128)(2,1)} %k_ref.2) | copy-start | bytes 196612
  2.0 11.4 %copy-start.2 = (bf16[256,128]{1,0:T(8,128)(2,1)S(1)}, bf16[256,128]{1,0:T(8,128)(2,1)}, u32[]{:S(2)}) copy-start(bf16[256,128]{1,0:T(8,128)(2,1)} %v_ref.2) | copy-start | bytes 196612
  2.0 14.5 %copy-start.4 = (bf16[4,512,128]{2,1,0:T(8,128)(2,1)S(1)}, bf16[4,512,128]{2,1,0:T(8,128)(2,1)}, u32[]{:S(2)}) copy-start(bf16[4,512,128]{2,1,0:T(8,128)(2,1)} %k_ref.3) | copy-start | bytes 1572868
  2.0 20.0 %all-to-all-start = ((bf16[32,4,512]{2,1,0:T(4,128)(2,1)}), bf16[32,4,512]{2,1,0:T(4,128)(2,1)S(1)}, u32[]{:S(2)}, u32[]{:S(2)}) async-start(bf16[32,4,512]{2,1,0:T(4,128)(2,1)} %get-tuple-element.12._), calls=%async_computation | async-start | bytes 262144 | tf_op jit(solution)/shard_map/all_to_all | solution.py:264
  13.6 8.4 %collective-permute-start = (bf16[1040,128]{1,0:T(8,128)(2,1)S(1)}, bf16[1040,128]{1,0:T(8,128)(2,1)S(1)}, u32[]{:S(2)}, u32[]{:S(2)}) collective-permute-start(bf16[1040,128]{1,0:T(8,128)(2,1)S(1)} %shard_map.123.own_ref.pack_ref), channel_id=1, source_target_pairs={{0,8},{8,0},{1,9},{9,1},{2,10},{10,2},{3,11},{11,3},{4,12},{12,4},... | collective-permute-start | bytes 798728 | tf_op jit(solution)/shard_map/ppermute | solution.py:282
  16.5 1.0 %copy-start.5 = (bf16[4,512,128]{2,1,0:T(8,128)(2,1)S(1)}, bf16[4,512,128]{2,1,0:T(8,128)(2,1)}, u32[]{:S(2)}) copy-start(bf16[4,512,128]{2,1,0:T(8,128)(2,1)} %v_ref.3) | copy-start | bytes 1572868
  52.4 13.9 %copy-start.6 = (bf16[256,512]{1,0:T(8,128)(2,1)S(1)}, bf16[256,512]{1,0:T(8,128)(2,1)}, u32[]{:S(2)}) copy-start(bf16[256,512]{1,0:T(8,128)(2,1)} %q_ref.3) | copy-start | bytes 786436
  53.2 20.2 %all-to-all-start.3 = ((bf16[16,16,128]{2,1,0:T(8,128)(2,1)}), bf16[16,16,128]{2,1,0:T(8,128)(2,1)S(1)}, u32[]{:S(2)}, u32[]{:S(2)}) async-start(bf16[16,16,128]{2,1,0:T(8,128)(2,1)} %bitcast.3._), calls=%async_computation.3 | async-start | bytes 131072 | tf_op jit(solution)/shard_map/all_to_all | solution.py:330

commit v6 on v5

--- a/solution.py
+++ b/solution.py
@@ -21,6 +21,7 @@
 bf16 = jnp.bfloat16
 vmem_limit = 32 * 1024 * 1024
 shadow_flops = 5 * 10**9
+first_chip, first_shard = 18, 5
 CH = 256
 at_requests, at_lengths, at_offset, at_core = 16, 32, 32 + REQ, 33 + REQ
 at_values, at_info, at_weight, at_end = CH, 2 * CH, 2 * CH + 16, 2 * CH + 16 + 512
@@ -48,6 +49,14 @@
 
 def dot(a, b, dims):
     return lax.dot_general(a, b, (dims, ((), ())), preferred_element_type=f32)
+
+
+def exchange(blocks, axes, first):
+    count = lax.axis_size(axes)
+    seats = [[(seat + first) % count for seat in range(count)]]
+    return lax.all_to_all(
+        blocks, axes, split_axis=0, concat_axis=0, axis_index_groups=seats, tiled=True
+    )
 
 
 def iota(shape, axis):
@@ -147,52 +156,67 @@
 
 
 def page_kernel(q_ref, own_ref, other_ref, out_ref):
-    core = own_ref[at_info:at_weight, :].astype(f32)[:, 3:4]
     pages = at_weight - at_info
     slots = out_ref.shape[0] * out_ref.shape[1]
-    placed = jnp.zeros((slots, out_ref.shape[2]), f32)
+    sides = (own_ref, other_ref)
+    info = jnp.concatenate([ref[at_info:at_weight, :].astype(f32) for ref in sides], axis=0)
+    group, request, earlier, core = info[:, 0:1], info[:, 1:2], info[:, 2:3], info[0:1, 3:4]
+    chip = jnp.floor(group * 0.5)
+    mine = group - 2.0 * chip == core
+    both = iota((2 * pages, 1), 0)
+    side = jnp.where(both < pages, 0.0, float(CAP))
+    seat = chip - first_chip
+    seat = jnp.where(seat < 0.0, seat + out_ref.shape[0], seat)
+    row = jnp.where(mine, seat * REQ + request, -1.0)
+    slot = jnp.where(mine, seat * (2 * CAP) + side + earlier, -1.0)
+    chosen = (iota((2 * pages, q_ref.shape[0]), 1).astype(f32) == row).astype(f32).astype(bf16)
+    placing = (iota((2 * pages, slots), 1).astype(f32) == slot).astype(f32).astype(bf16)
+    asked = dot(chosen, q_ref[...], ((1,), (0,)))
     own = iota((QPK * pages, CH), 1) // PAGE == iota((QPK * pages, CH), 0) % pages
+    wide_lane, wide_row = iota((QPK * pages, HD), 1), iota((QPK * pages, HD), 0)
+    spot = jnp.where(wide_lane // REQ % QPK == wide_row // pages, wide_lane // ROWS, -1)
     lane = iota((pages, HD), 1)
-    row_lane = iota((pages, q_ref.shape[0]), 1).astype(f32)
-    slot_lane = iota((pages, slots), 1).astype(f32)
-    for side, ref in enumerate((own_ref, other_ref)):
-        info = ref[at_info:at_weight, :].astype(f32)
-        group, request, earlier = info[:, 0:1], info[:, 1:2], info[:, 2:3]
-        chip = jnp.floor(group * 0.5)
-        mine = group - 2.0 * chip == core
-        row = jnp.where(mine, chip * REQ + request, -1.0)
-        slot = jnp.where(mine, chip * (2 * CAP) + side * CAP + earlier, -1.0)
-        chosen = (row_lane == row).astype(f32).astype(bf16)
-        placing = (slot_lane == slot).astype(f32).astype(bf16)
-        asked = dot(chosen, q_ref[...], ((1,), (0,)))
-        asked = [asked[:, h * HD : (h + 1) * HD] for h in range(QPK)]
-        queries = jnp.concatenate(asked, axis=0).astype(bf16)
+    payload = []
+    for i, ref in enumerate(sides):
+        here = slice(i * pages, (i + 1) * pages)
+        queries = [asked[here, h * HD : (h + 1) * HD] for h in range(QPK)]
+        queries = jnp.concatenate(queries, axis=0).astype(bf16)
         scores = dot(queries, ref[:at_values, :], ((1,), (1,))) * scale
         scores = jnp.where(own, scores, neg_large)
         peak = jnp.max(scores, axis=1, keepdims=True)
         weights = jnp.where(own, jnp.exp(scores - peak), 0.0)
         total = jnp.sum(weights, axis=1, keepdims=True)
         values = dot(weights.astype(bf16), ref[at_values:at_info, :], ((1,), (0,))) / total
-        extra = jnp.where(lane // ROWS == 5, request + 1.0, 0.0)
-        parts = parts_of(peak, 3) + parts_of(total, 2)
+        wide = jnp.zeros((QPK * pages, HD), f32)
+        for block, column in enumerate(parts_of(peak, 3) + parts_of(total, 2)):
+            wide = jnp.where(spot == block, column, wide)
+        extra = jnp.where(lane // ROWS == 5, request[here] + 1.0, 0.0)
         columns = []
         for h in range(QPK):
             part = slice(h * pages, (h + 1) * pages)
             columns.append(values[part])
-            for block, column in enumerate(parts):
-                extra = jnp.where(lane // REQ == block * QPK + h, column[part], extra)
-        payload = jnp.concatenate(columns + [extra], axis=1).astype(bf16)
-        placed = placed + dot(placing, payload, ((0,), (0,)))
+            extra = extra + wide[part]
+        payload.append(jnp.concatenate(columns + [extra], axis=1))
+    payload = jnp.concatenate(payload, axis=0).astype(bf16)
+    placed = dot(placing, payload, ((0,), (0,)))
     out_ref[...] = placed.reshape(out_ref.shape).astype(bf16)
 
 
 def project_kernel(rows_ref, own_ref, other_ref, out_ref):
     first = own_ref[at_info : at_info + 16, :].astype(f32)[0:1, 3:4] == 0.0
     rows = rows_ref[...]
-    own = dot(rows, own_ref[at_weight:, :], ((1,), (0,)))
-    other = dot(rows, other_ref[at_weight:, :], ((1,), (0,)))
-    out_ref[0] = jnp.where(first, own, other).astype(bf16)
-    out_ref[1] = jnp.where(first, other, own).astype(bf16)
+    start = rows.shape[0] - first_chip * REQ
+
+    def product(weight):
+        terms = dot(rows, weight, ((1,), (0,)))
+        return jnp.concatenate([terms[start:], terms[:start]], axis=0)
+
+    own, other = product(own_ref[at_weight:, :]), product(other_ref[at_weight:, :])
+    blocks = jnp.where(first, own, other).astype(bf16), jnp.where(first, other, own).astype(bf16)
+    count, height = out_ref.shape[0], out_ref.shape[1]
+    for seat in range(count):
+        c, z = divmod((seat + first_shard) % count, count // 2)
+        out_ref[seat] = blocks[c][z * height : (z + 1) * height]
 
 
 def combine_kernel(got_ref, sum_ref, peak_ref, total_ref, out_ref):
@@ -223,12 +247,13 @@
 
 
 def sum_kernel(terms_ref, out_ref):
-    half = terms_ref.shape[0] // 2
+    count = terms_ref.shape[0]
+    half = count // 2
     sums = []
     for c in range(2):
-        total = terms_ref[c * half].astype(f32)
+        total = terms_ref[(c * half - first_shard) % count].astype(f32)
         for t in range(1, half):
-            total = total + terms_ref[c * half + t].astype(f32)
+            total = total + terms_ref[(c * half + t - first_shard) % count].astype(f32)
         sums.append(total)
     blocks = []
     for x in range(terms_ref.shape[1] // REQ):
@@ -261,7 +286,7 @@
         ),
         decode_q,
     )
-    asked = lax.all_to_all(asking, chips, split_axis=0, concat_axis=0, tiled=True)
+    asked = exchange(asking, chips, first_chip)
     asked = asked.reshape(peers * REQ, width)
 
     core = lax.axis_index("c").reshape(1)
@@ -299,24 +324,23 @@
         own,
         other,
     )
-    got = lax.all_to_all(sent, chips, split_axis=0, concat_axis=0, tiled=True)
+    got = exchange(sent, chips, first_chip)
     got = got.reshape(peers * 2 * CAP, width + HD)
 
     repeated = call(
         combine_kernel, jax.ShapeDtypeStruct((peers, REQ, width), bf16), got, *home
     )
-    everyone = lax.all_to_all(repeated, chips, split_axis=0, concat_axis=0, tiled=True)
+    everyone = exchange(repeated, chips, first_chip)
     everyone = everyone.reshape(peers * REQ, width)
     shards = lax.axis_size("z")
     cores = lax.axis_size("c")
     terms = call(
         project_kernel,
-        jax.ShapeDtypeStruct((cores, peers * REQ, HD), bf16),
+        jax.ShapeDtypeStruct((cores * shards, peers * REQ // shards, HD), bf16),
         everyone,
         own,
         other,
     )
-    terms = terms.reshape(cores * shards, peers * REQ // shards, HD)
     prefill_out = call(
         prefill_kernel,
         jax.ShapeDtypeStruct(prefill_q.shape, bf16),
@@ -327,7 +351,7 @@
         unread=1,
         flops=shadow_flops,
     )
-    terms = lax.all_to_all(terms, ("c", "z"), split_axis=0, concat_axis=0, tiled=True)
+    terms = exchange(terms, ("c", "z"), first_shard)
     decode_out = call(
         sum_kernel, jax.ShapeDtypeStruct((peers * REQ * cores // shards, HD), bf16), terms
     )

time: 74.4 us -> 67.6 us (0.909)
  waiting for transfers between devices: 9.17 us -> 1.97 us
  starting transfers between devices: 26.5 us -> 29.8 us
  blocking collectives: 28.6 us -> 25.9 us
    all_to_all x2, waiting for transfers between devices: 9.16 us -> 1.96 us  [exchange(): lax.all_to_all(blocks, axes, split_axis=0, concat_axis=0, axis_index_grou...]
    ppermute x1, starting transfers between devices: 2.86 us -> 6.12 us  [on_device(): other = lax.ppermute(own, 'c', [(0, 1), (1, 0)])]
    all_to_all x2, blocking collectives: 28.6 us -> 25.9 us  [exchange(): lax.all_to_all(blocks, axes, split_axis=0, concat_axis=0, axis_index_grou...]
  transfers between devices with their start and end apart: 3 -> 3, of which waited for: 2 -> 1; matrix products, arithmetic and copies ran while one was open for 0% -> 0% of each run, Pallas kernels for 4% -> 4%
where the time goes in v6:
time: 67.6 us; the launch traced here: 67.1 us
  starting transfers between devices  29.8 us (44%)
  blocking collectives  25.9 us (38%)
  Pallas kernels  6.13 us (9%)
  waiting for transfers between devices  1.97 us (3%)
  local copies, waits for them, and re-layouts  1.86 us (3%)
  between operations  1.42 us (2%)
    all_to_all x2, blocking collectives, exchange(): lax.all_to_all(blocks, axes, split_axis=0, concat_axis=0, axis_index_grou...  25.9 us
    all_to_all x2, starting transfers between devices, exchange(): lax.all_to_all(blocks, axes, split_axis=0, concat_axis=0, axis_index_grou...  23.7 us
    pallas_call x8, Pallas kernels, call(): pl.pallas_call(kernel, out_shape=outs, in_specs=[pl.BlockSpec(memory_spac...  6.13 us
    ppermute x1, starting transfers between devices, on_device(): other = lax.ppermute(own, 'c', [(0, 1), (1, 0)])  6.12 us
    all_to_all x2, waiting for transfers between devices, exchange(): lax.all_to_all(blocks, axes, split_axis=0, concat_axis=0, axis_index_grou...  1.96 us
    unnamed x20, local copies, waits for them, and re-layouts  1.75 us
  transfers between devices with their start and end apart: 3, of which 1 were waited for; matrix products, arithmetic and copies ran while one was open for 0% of the time, Pallas kernels for 4%

profile of v6, /device:TPU:1, one launch (start us, length us, event | category | flops | bytes accessed | tf_op | source)
XLA Modules:
  0.0 67.1 jit_solution(3509659198225923351)
XLA Ops:
  0.6 0.0 copy-start.3
  0.6 0.7 %copy-done.3 = bf16[4,512]{1,0:T(4,128)(2,1)S(1)} copy-done((bf16[4,512]{1,0:T(4,128)(2,1)S(1)}, bf16[4,512]{1,0:T(4,128)(2,1)}, u32[]{:S(2)}) %copy-start.3) | copy-done | bytes 4120
  1.3 0.0 copy-start.7
  1.3 0.0 copy-start.8
  1.3 0.0 copy-start.9
  1.3 0.7 shard_map.122
  2.0 0.0 copy-start
  2.0 0.0 copy-start.1
  2.0 0.0 copy-start.2
  2.0 0.0 copy-start.4
  2.0 12.6 %all-to-all-start = ((bf16[32,4,512]{2,1,0:T(4,128)(2,1)}), bf16[32,4,512]{2,1,0:T(4,128)(2,1)S(1)}, u32[]{:S(2)}, u32[]{:S(2)}) async-start(bf16[32,4,512]{2,1,0:T(4,128)(2,1)} %get-tuple-element.12._), calls=%async_computation | async-start | bytes 262144 | tf_op jit(solution)/shard_map/all_to_all | solution.py:57
  15.2 0.0 copy-done.7
  15.2 0.0 copy-done.8
  15.3 0.0 copy-done.9
  15.3 0.1 add_bitcast_fusion.ints_ref
  15.3 0.0 copy-done
  15.4 0.0 copy-done.1
  15.4 0.0 copy-done.2
  15.4 0.2 shard_map.123.own_ref.pack_ref
  15.5 6.1 %collective-permute-start = (bf16[1040,128]{1,0:T(8,128)(2,1)S(1)}, bf16[1040,128]{1,0:T(8,128)(2,1)S(1)}, u32[]{:S(2)}, u32[]{:S(2)}) collective-permute-start(bf16[1040,128]{1,0:T(8,128)(2,1)S(1)} %shard_map.123.own_ref.pack_ref), channel_id=1, source_target_pairs={{0,8},{8,0},{1,9},{9,1},{2,10},{10,2},{3,11},{11,3},{4,12},{12,4},... | collective-permute-start | bytes 798728 | tf_op jit(solution)/shard_map/ppermute | solution.py:307
  21.7 0.0 copy-done.4
  21.7 0.0 copy-start.5
  21.7 1.0 %copy-done.5 = bf16[4,512,128]{2,1,0:T(8,128)(2,1)S(1)} copy-done((bf16[4,512,128]{2,1,0:T(8,128)(2,1)S(1)}, bf16[4,512,128]{2,1,0:T(8,128)(2,1)}, u32[]{:S(2)}) %copy-start.5) | copy-done | bytes 524312
  22.7 0.5 shard_map.124
  23.3 0.0 all-to-all-done
  23.3 0.0 collective-permute-done.other_ref
  23.3 1.0 %shard_map.125 = bf16[32,4,640]{2,1,0:T(4,128)(2,1)S(1)} custom-call(bf16[128,512]{1,0:T(8,128)(2,1)S(1)} %reshape.21.q_ref, bf16[1040,128]{1,0:T(8,128)(2,1)S(1)} %shard_map.123.own_ref.pack_ref, bf16[1040,128]{1,0:T(8,128)(2,1)S(1)} %collective-permute-done.other_ref), custom_call_target="tpu_custom_call" | custom-call | bytes 827392 | tf_op jit(solution)/shard_map/pallas_call | solution.py:69
  24.3 13.8 %all_to_all.20 = bf16[32,4,640]{2,1,0:T(4,128)(2,1)S(1)} all-to-all(bf16[32,4,640]{2,1,0:T(4,128)(2,1)S(1)} %shard_map.125), channel_id=1, replica_groups={{288,304,320,336,352,368,384,400,416,432,448,464,480,496,0,16,32,48,64,..., dimensions={0} | all-to-all | bytes 327680 | tf_op jit(solution)/shard_map/all_to_all | solution.py:57
  38.2 0.3 shard_map.126
  38.5 12.1 %all_to_all.21 = bf16[32,4,512]{2,1,0:T(4,128)(2,1)S(1)} all-to-all(bf16[32,4,512]{2,1,0:T(4,128)(2,1)S(1)} %shard_map.126), channel_id=1, replica_groups={{288,304,320,336,352,368,384,400,416,432,448,464,480,496,0,16,32,48,64,..., dimensions={0} | all-to-all | bytes 262144 | tf_op jit(solution)/shard_map/all_to_all | solution.py:57
  50.6 0.0 copy-start.6
  50.7 0.9 %shard_map.127._ = bf16[16,16,128]{2,1,0:T(8,128)(2,1)} custom-call(bf16[128,512]{1,0:T(8,128)(2,1)S(1)} %reshape.23.rows_ref, bf16[1040,128]{1,0:T(8,128)(2,1)S(1)} %shard_map.123.own_ref.pack_ref, bf16[1040,128]{1,0:T(8,128)(2,1)S(1)} %collective-permute-done.other_ref), custom_call_target="tpu_custom_call" | custom-call | bytes 729088 | tf_op jit(solution)/shard_map/pallas_call | solution.py:69
  51.5 11.1 %all-to-all-start.3 = ((bf16[16,16,128]{2,1,0:T(8,128)(2,1)}), bf16[16,16,128]{2,1,0:T(8,128)(2,1)S(1)}, u32[]{:S(2)}, u32[]{:S(2)}) async-start(bf16[16,16,128]{2,1,0:T(8,128)(2,1)} %shard_map.127._), calls=%async_computation.3 | async-start | bytes 131072 | tf_op jit(solution)/shard_map/all_to_all | solution.py:57
  62.6 0.0 copy-done.6
  62.6 1.9 %shard_map.128 = bf16[256,512]{1,0:T(8,128)(2,1)} custom-call(s32[1,128]{1,0:T(1,128)S(1)} %add_bitcast_fusion.ints_ref, bf16[256,512]{1,0:T(8,128)(2,1)S(1)} %copy-done.6, bf16[1040,128]{1,0:T(8,128)(2,1)S(1)} %shard_map.123.own_ref.pack_ref, bf16[16,16,128]{2,1,0:T(8,128)(2,1)} %shard_map.127._), custom_call_target="tpu_custom_call" | custom-call | flops 5000000000 | bytes 856576 | tf_op jit(solution)/shard_map/pallas_call | solution.py:69
  64.6 2.0 %all-to-all-done.3.terms_ref = bf16[16,16,128]{2,1,0:T(8,128)(2,1)S(1)} async-done(((bf16[16,16,128]{2,1,0:T(8,128)(2,1)}), bf16[16,16,128]{2,1,0:T(8,128)(2,1)S(1)}, u32[]{:S(2)}, u32[]{:S(2)}) %all-to-all-start.3) | async-done | bytes 65568 | tf_op jit(solution)/shard_map/all_to_all | solution.py:57
  66.5 0.6 shard_map.129
  (3 shorter events, 0.1 us)
Async XLA Ops:
  0.6 0.7 %copy-start.3 = (bf16[4,512]{1,0:T(4,128)(2,1)S(1)}, bf16[4,512]{1,0:T(4,128)(2,1)}, u32[]{:S(2)}) copy-start(bf16[4,512]{1,0:T(4,128)(2,1)} %q_ref.2) | copy-start | bytes 12292
  1.3 13.9 %copy-start.7 = (s32[4]{0:T(128)S(1)}, s32[4]{0:T(128)}, u32[]{:S(2)}) copy-start(s32[4]{0:T(128)} %param.20) | copy-start | bytes 52
  1.3 13.9 %copy-start.8 = (s32[16]{0:T(128)S(1)}, s32[16]{0:T(128)}, u32[]{:S(2)}) copy-start(s32[16]{0:T(128)} %param.16) | copy-start | bytes 196
  1.3 13.9 %copy-start.9 = (s32[16,1]{0,1:T(1,128)S(1)}, s32[16,1]{0,1:T(1,128)}, u32[]{:S(2)}) copy-start(s32[16,1]{0,1:T(1,128)} %param.15) | copy-start | bytes 196
  2.0 13.4 %copy-start = (bf16[512,128]{1,0:T(8,128)(2,1)S(1)}, bf16[512,128]{1,0:T(8,128)(2,1)}, u32[]{:S(2)}) copy-start(bf16[512,128]{1,0:T(8,128)(2,1)} %weight_ref.1) | copy-start | bytes 393220
  2.0 13.4 %copy-start.1 = (bf16[256,128]{1,0:T(8,128)(2,1)S(1)}, bf16[256,128]{1,0:T(8,128)(2,1)}, u32[]{:S(2)}) copy-start(bf16[256,128]{1,0:T(8,128)(2,1)} %k_ref.2) | copy-start | bytes 196612
  2.0 13.4 %copy-start.2 = (bf16[256,128]{1,0:T(8,128)(2,1)S(1)}, bf16[256,128]{1,0:T(8,128)(2,1)}, u32[]{:S(2)}) copy-start(bf16[256,128]{1,0:T(8,128)(2,1)} %v_ref.2) | copy-start | bytes 196612
  2.0 19.7 %copy-start.4 = (bf16[4,512,128]{2,1,0:T(8,128)(2,1)S(1)}, bf16[4,512,128]{2,1,0:T(8,128)(2,1)}, u32[]{:S(2)}) copy-start(bf16[4,512,128]{2,1,0:T(8,128)(2,1)} %k_ref.3) | copy-start | bytes 1572868
  2.0 21.3 %all-to-all-start = ((bf16[32,4,512]{2,1,0:T(4,128)(2,1)}), bf16[32,4,512]{2,1,0:T(4,128)(2,1)S(1)}, u32[]{:S(2)}, u32[]{:S(2)}) async-start(bf16[32,4,512]{2,1,0:T(4,128)(2,1)} %get-tuple-element.12._), calls=%async_computation | async-start | bytes 262144 | tf_op jit(solution)/shard_map/all_to_all | solution.py:57
  15.5 7.8 %collective-permute-start = (bf16[1040,128]{1,0:T(8,128)(2,1)S(1)}, bf16[1040,128]{1,0:T(8,128)(2,1)S(1)}, u32[]{:S(2)}, u32[]{:S(2)}) collective-permute-start(bf16[1040,128]{1,0:T(8,128)(2,1)S(1)} %shard_map.123.own_ref.pack_ref), channel_id=1, source_target_pairs={{0,8},{8,0},{1,9},{9,1},{2,10},{10,2},{3,11},{11,3},{4,12},{12,4},... | collective-permute-start | bytes 798728 | tf_op jit(solution)/shard_map/ppermute | solution.py:307
  21.7 1.0 %copy-start.5 = (bf16[4,512,128]{2,1,0:T(8,128)(2,1)S(1)}, bf16[4,512,128]{2,1,0:T(8,128)(2,1)}, u32[]{:S(2)}) copy-start(bf16[4,512,128]{2,1,0:T(8,128)(2,1)} %v_ref.3) | copy-start | bytes 1572868
  50.6 12.0 %copy-start.6 = (bf16[256,512]{1,0:T(8,128)(2,1)S(1)}, bf16[256,512]{1,0:T(8,128)(2,1)}, u32[]{:S(2)}) copy-start(bf16[256,512]{1,0:T(8,128)(2,1)} %q_ref.3) | copy-start | bytes 786436
  51.5 15.0 %all-to-all-start.3 = ((bf16[16,16,128]{2,1,0:T(8,128)(2,1)}), bf16[16,16,128]{2,1,0:T(8,128)(2,1)S(1)}, u32[]{:S(2)}, u32[]{:S(2)}) async-start(bf16[16,16,128]{2,1,0:T(8,128)(2,1)} %shard_map.127._), calls=%async_computation.3 | async-start | bytes 131072 | tf_op jit(solution)/shard_map/all_to_all | solution.py:57

commit v7 on v6

--- a/solution.py
+++ b/solution.py
@@ -21,7 +21,7 @@
 bf16 = jnp.bfloat16
 vmem_limit = 32 * 1024 * 1024
 shadow_flops = 5 * 10**9
-first_chip, first_shard = 18, 5
+first_chip, first_shard = 18, 4
 CH = 256
 at_requests, at_lengths, at_offset, at_core = 16, 32, 32 + REQ, 33 + REQ
 at_values, at_info, at_weight, at_end = CH, 2 * CH, 2 * CH + 16, 2 * CH + 16 + 512
@@ -116,7 +116,7 @@
         out_ref[:, part] = dot(weights.astype(bf16), values, ((1,), (0,))).astype(bf16)
 
 
-def resident_kernel(rows_ref, k_ref, v_ref, ints_ref, sum_ref, peak_ref, total_ref):
+def resident_kernel(rows_ref, k_ref, ints_ref, low_ref, peak_ref, total_ref):
     rows = rows_ref[...]
     slots = k_ref.shape[1]
     request = iota((ROWS, 1), 0) % REQ
@@ -130,11 +130,7 @@
     peak = jnp.max(scores, axis=1, keepdims=True)
     weights = jnp.where(shown, jnp.exp(scores - peak), 0.0)
     total = jnp.sum(weights, axis=1, keepdims=True)
-    low = weights.astype(bf16)
-    summed = jnp.zeros((ROWS, HD), f32)
-    for r in range(REQ):
-        summed = jnp.where(request == r, dot(low, v_ref[r], ((1,), (0,))), summed)
-    sum_ref[...] = summed
+    low_ref[...] = weights.astype(bf16)
     peak_ref[...] = jnp.broadcast_to(peak, (ROWS, HD))
     total_ref[...] = jnp.broadcast_to(total, (ROWS, HD))
 
@@ -219,7 +215,7 @@
         out_ref[seat] = blocks[c][z * height : (z + 1) * height]
 
 
-def combine_kernel(got_ref, sum_ref, peak_ref, total_ref, out_ref):
+def combine_kernel(got_ref, low_ref, peak_ref, total_ref, v_ref, out_ref):
     slots = got_ref.shape[0]
     extra = got_ref[:, QPK * HD :].astype(f32)
     block = [extra] + [pltpu.roll(extra, HD - ROWS * i, 1) for i in range(1, 6)]
@@ -237,7 +233,12 @@
     whole = jnp.where(iota((1, HD), 1) < ROWS, whole, 1.0)
     low = (weights / whole).astype(bf16)[:, :ROWS]
     home_column = jnp.sum(jnp.where(eye, home / whole, 0.0), axis=1, keepdims=True)
-    rows = sum_ref[...] * home_column
+    summed = jnp.zeros((ROWS, HD), f32)
+    request = iota((ROWS, 1), 0) % REQ
+    for r in range(REQ):
+        add = dot(low_ref[...], v_ref[r], ((1,), (0,)))
+        summed = jnp.where(request == r, add, summed)
+    rows = summed * home_column
     head = iota((ROWS, HD), 0) // REQ
     for h in range(QPK):
         add = dot(low, got_ref[:, h * HD : (h + 1) * HD], ((0,), (0,)))
@@ -309,10 +310,9 @@
     rows_of = jax.ShapeDtypeStruct((ROWS, HD), f32)
     home = call(
         resident_kernel,
-        (rows_of,) * 3,
+        (jax.ShapeDtypeStruct((ROWS, cache_k.shape[1]), bf16), rows_of, rows_of),
         rows,
         cache_k,
-        cache_v,
         ints,
         flops=shadow_flops,
     )
@@ -328,7 +328,7 @@
     got = got.reshape(peers * 2 * CAP, width + HD)
 
     repeated = call(
-        combine_kernel, jax.ShapeDtypeStruct((peers, REQ, width), bf16), got, *home
+        combine_kernel, jax.ShapeDtypeStruct((peers, REQ, width), bf16), got, *home, cache_v
     )
     everyone = exchange(repeated, chips, first_chip)
     everyone = everyone.reshape(peers * REQ, width)

time: 67.6 us -> 67 us (level)
  starting transfers between devices: 29.8 us -> 30.9 us
  local copies, waits for them, and re-layouts: 1.86 us -> 0.83 us
    all_to_all x2, waiting for transfers between devices: 1.96 us -> 0.9 us  [exchange(): lax.all_to_all(blocks, axes, split_axis=0, concat_axis=0, axis_index_grou...]
    all_to_all x2, starting transfers between devices: 23.7 us -> 24.7 us  [exchange(): lax.all_to_all(blocks, axes, split_axis=0, concat_axis=0, axis_index_grou...]
    unnamed x20, local copies, waits for them, and re-layouts: 1.75 us -> 0.72 us
  transfers between devices with their start and end apart: 3 -> 3, of which waited for: 1 -> 2; matrix products, arithmetic and copies ran while one was open for 0% -> 0% of each run, Pallas kernels for 4% -> 4%
where the time goes in v7:
time: 67 us; the launch traced here: 66.7 us
  starting transfers between devices  30.9 us (46%)
  blocking collectives  25.9 us (39%)
  Pallas kernels  6.05 us (9%)
  waiting for transfers between devices  1.55 us (2%)
  between operations  1.42 us (2%)
  local copies, waits for them, and re-layouts  0.83 us (1%)
    all_to_all x2, blocking collectives, exchange(): lax.all_to_all(blocks, axes, split_axis=0, concat_axis=0, axis_index_grou...  25.9 us
    all_to_all x2, starting transfers between devices, exchange(): lax.all_to_all(blocks, axes, split_axis=0, concat_axis=0, axis_index_grou...  24.7 us
    ppermute x1, starting transfers between devices, on_device(): other = lax.ppermute(own, 'c', [(0, 1), (1, 0)])  6.12 us
    pallas_call x8, Pallas kernels, call(): pl.pallas_call(kernel, out_shape=outs, in_specs=[pl.BlockSpec(memory_spac...  6.05 us
  transfers between devices with their start and end apart: 3, of which 2 were waited for; matrix products, arithmetic and copies ran while one was open for 0% of the time, Pallas kernels for 4%

profile of v7, /device:TPU:1, one launch (start us, length us, event | category | flops | bytes accessed | tf_op | source)
XLA Modules:
  0.0 66.7 jit_solution(4430039273023391423)
XLA Ops:
  0.6 0.0 copy-start.4
  0.6 0.7 %copy-done.4 = bf16[4,512]{1,0:T(4,128)(2,1)S(1)} copy-done((bf16[4,512]{1,0:T(4,128)(2,1)S(1)}, bf16[4,512]{1,0:T(4,128)(2,1)}, u32[]{:S(2)}) %copy-start.4) | copy-done | bytes 4120
  1.3 0.0 copy-start.7
  1.3 0.0 copy-start.8
  1.3 0.0 copy-start.9
  1.3 0.7 shard_map.122
  2.0 0.0 copy-start.1
  2.0 0.0 copy-start.2
  2.0 0.0 copy-start.3
  2.0 0.0 copy-start.5
  2.0 12.6 %all-to-all-start = ((bf16[32,4,512]{2,1,0:T(4,128)(2,1)}), bf16[32,4,512]{2,1,0:T(4,128)(2,1)S(1)}, u32[]{:S(2)}, u32[]{:S(2)}) async-start(bf16[32,4,512]{2,1,0:T(4,128)(2,1)} %get-tuple-element.12._), calls=%async_computation | async-start | bytes 262144 | tf_op jit(solution)/shard_map/all_to_all | solution.py:57
  15.2 0.0 copy-done.7
  15.2 0.0 copy-done.8
  15.3 0.0 copy-done.9
  15.3 0.1 add_bitcast_fusion.ints_ref
  15.3 0.0 copy-done.1
  15.4 0.0 copy-done.2
  15.4 0.0 copy-done.3
  15.4 0.2 shard_map.123.own_ref.pack_ref
  15.5 6.1 %collective-permute-start = (bf16[1040,128]{1,0:T(8,128)(2,1)S(1)}, bf16[1040,128]{1,0:T(8,128)(2,1)S(1)}, u32[]{:S(2)}, u32[]{:S(2)}) collective-permute-start(bf16[1040,128]{1,0:T(8,128)(2,1)S(1)} %shard_map.123.own_ref.pack_ref), channel_id=1, source_target_pairs={{0,8},{8,0},{1,9},{9,1},{2,10},{10,2},{3,11},{11,3},{4,12},{12,4},... | collective-permute-start | bytes 798728 | tf_op jit(solution)/shard_map/ppermute | solution.py:308
  21.7 0.0 copy-done.5
  21.7 0.4 shard_map.124
  22.1 0.0 all-to-all-done
  22.2 0.6 collective-permute-done.other_ref
  22.8 1.0 %shard_map.125 = bf16[32,4,640]{2,1,0:T(4,128)(2,1)S(1)} custom-call(bf16[128,512]{1,0:T(8,128)(2,1)S(1)} %reshape.21.q_ref, bf16[1040,128]{1,0:T(8,128)(2,1)S(1)} %shard_map.123.own_ref.pack_ref, bf16[1040,128]{1,0:T(8,128)(2,1)S(1)} %collective-permute-done.other_ref), custom_call_target="tpu_custom_call" | custom-call | bytes 827392 | tf_op jit(solution)/shard_map/pallas_call | solution.py:69
  23.8 0.0 copy-start
  23.9 13.8 %all_to_all.20 = bf16[32,4,640]{2,1,0:T(4,128)(2,1)S(1)} all-to-all(bf16[32,4,640]{2,1,0:T(4,128)(2,1)S(1)} %shard_map.125), channel_id=1, replica_groups={{288,304,320,336,352,368,384,400,416,432,448,464,480,496,0,16,32,48,64,..., dimensions={0} | all-to-all | bytes 327680 | tf_op jit(solution)/shard_map/all_to_all | solution.py:57
  37.7 0.0 copy-done
  37.7 0.3 shard_map.126
  38.0 12.1 %all_to_all.21 = bf16[32,4,512]{2,1,0:T(4,128)(2,1)S(1)} all-to-all(bf16[32,4,512]{2,1,0:T(4,128)(2,1)S(1)} %shard_map.126), channel_id=1, replica_groups={{288,304,320,336,352,368,384,400,416,432,448,464,480,496,0,16,32,48,64,..., dimensions={0} | all-to-all | bytes 262144 | tf_op jit(solution)/shard_map/all_to_all | solution.py:57
  50.2 0.0 copy-start.6
  50.2 0.9 %shard_map.127._ = bf16[16,16,128]{2,1,0:T(8,128)(2,1)} custom-call(bf16[128,512]{1,0:T(8,128)(2,1)S(1)} %reshape.23.rows_ref, bf16[1040,128]{1,0:T(8,128)(2,1)S(1)} %shard_map.123.own_ref.pack_ref, bf16[1040,128]{1,0:T(8,128)(2,1)S(1)} %collective-permute-done.other_ref), custom_call_target="tpu_custom_call" | custom-call | bytes 729088 | tf_op jit(solution)/shard_map/pallas_call | solution.py:69
  51.0 12.2 %all-to-all-start.3 = ((bf16[16,16,128]{2,1,0:T(8,128)(2,1)}), bf16[16,16,128]{2,1,0:T(8,128)(2,1)S(1)}, u32[]{:S(2)}, u32[]{:S(2)}) async-start(bf16[16,16,128]{2,1,0:T(8,128)(2,1)} %shard_map.127._), calls=%async_computation.3 | async-start | bytes 131072 | tf_op jit(solution)/shard_map/all_to_all | solution.py:57
  63.2 0.0 copy-done.6
  63.2 1.9 %shard_map.128 = bf16[256,512]{1,0:T(8,128)(2,1)} custom-call(s32[1,128]{1,0:T(1,128)S(1)} %add_bitcast_fusion.ints_ref, bf16[256,512]{1,0:T(8,128)(2,1)S(1)} %copy-done.6, bf16[1040,128]{1,0:T(8,128)(2,1)S(1)} %shard_map.123.own_ref.pack_ref, bf16[16,16,128]{2,1,0:T(8,128)(2,1)} %shard_map.127._), custom_call_target="tpu_custom_call" | custom-call | flops 5000000000 | bytes 856576 | tf_op jit(solution)/shard_map/pallas_call | solution.py:69
  65.1 0.9 %all-to-all-done.3.terms_ref = bf16[16,16,128]{2,1,0:T(8,128)(2,1)S(1)} async-done(((bf16[16,16,128]{2,1,0:T(8,128)(2,1)}), bf16[16,16,128]{2,1,0:T(8,128)(2,1)S(1)}, u32[]{:S(2)}, u32[]{:S(2)}) %all-to-all-start.3) | async-done | bytes 65568 | tf_op jit(solution)/shard_map/all_to_all | solution.py:57
  66.0 0.6 shard_map.129
  (3 shorter events, 0.1 us)
Async XLA Ops:
  0.6 0.7 %copy-start.4 = (bf16[4,512]{1,0:T(4,128)(2,1)S(1)}, bf16[4,512]{1,0:T(4,128)(2,1)}, u32[]{:S(2)}) copy-start(bf16[4,512]{1,0:T(4,128)(2,1)} %q_ref.2) | copy-start | bytes 12292
  1.3 13.9 %copy-start.7 = (s32[4]{0:T(128)S(1)}, s32[4]{0:T(128)}, u32[]{:S(2)}) copy-start(s32[4]{0:T(128)} %param.20) | copy-start | bytes 52
  1.3 13.9 %copy-start.8 = (s32[16]{0:T(128)S(1)}, s32[16]{0:T(128)}, u32[]{:S(2)}) copy-start(s32[16]{0:T(128)} %param.16) | copy-start | bytes 196
  1.3 13.9 %copy-start.9 = (s32[16,1]{0,1:T(1,128)S(1)}, s32[16,1]{0,1:T(1,128)}, u32[]{:S(2)}) copy-start(s32[16,1]{0,1:T(1,128)} %param.15) | copy-start | bytes 196
  2.0 13.4 %copy-start.1 = (bf16[512,128]{1,0:T(8,128)(2,1)S(1)}, bf16[512,128]{1,0:T(8,128)(2,1)}, u32[]{:S(2)}) copy-start(bf16[512,128]{1,0:T(8,128)(2,1)} %weight_ref.1) | copy-start | bytes 393220
  2.0 13.4 %copy-start.2 = (bf16[256,128]{1,0:T(8,128)(2,1)S(1)}, bf16[256,128]{1,0:T(8,128)(2,1)}, u32[]{:S(2)}) copy-start(bf16[256,128]{1,0:T(8,128)(2,1)} %k_ref.2) | copy-start | bytes 196612
  2.0 13.4 %copy-start.3 = (bf16[256,128]{1,0:T(8,128)(2,1)S(1)}, bf16[256,128]{1,0:T(8,128)(2,1)}, u32[]{:S(2)}) copy-start(bf16[256,128]{1,0:T(8,128)(2,1)} %v_ref.2) | copy-start | bytes 196612
  2.0 19.7 %copy-start.5 = (bf16[4,512,128]{2,1,0:T(8,128)(2,1)S(1)}, bf16[4,512,128]{2,1,0:T(8,128)(2,1)}, u32[]{:S(2)}) copy-start(bf16[4,512,128]{2,1,0:T(8,128)(2,1)} %k_ref.3) | copy-start | bytes 1572868
  2.0 20.1 %all-to-all-start = ((bf16[32,4,512]{2,1,0:T(4,128)(2,1)}), bf16[32,4,512]{2,1,0:T(4,128)(2,1)S(1)}, u32[]{:S(2)}, u32[]{:S(2)}) async-start(bf16[32,4,512]{2,1,0:T(4,128)(2,1)} %get-tuple-element.12._), calls=%async_computation | async-start | bytes 262144 | tf_op jit(solution)/shard_map/all_to_all | solution.py:57
  15.5 7.3 %collective-permute-start = (bf16[1040,128]{1,0:T(8,128)(2,1)S(1)}, bf16[1040,128]{1,0:T(8,128)(2,1)S(1)}, u32[]{:S(2)}, u32[]{:S(2)}) collective-permute-start(bf16[1040,128]{1,0:T(8,128)(2,1)S(1)} %shard_map.123.own_ref.pack_ref), channel_id=1, source_target_pairs={{0,8},{8,0},{1,9},{9,1},{2,10},{10,2},{3,11},{11,3},{4,12},{12,4},... | collective-permute-start | bytes 798728 | tf_op jit(solution)/shard_map/ppermute | solution.py:308
  23.8 13.8 %copy-start = (bf16[4,512,128]{2,1,0:T(8,128)(2,1)S(1)}, bf16[4,512,128]{2,1,0:T(8,128)(2,1)}, u32[]{:S(2)}) copy-start(bf16[4,512,128]{2,1,0:T(8,128)(2,1)} %v_ref.3) | copy-start | bytes 1572868
  50.2 13.0 %copy-start.6 = (bf16[256,512]{1,0:T(8,128)(2,1)S(1)}, bf16[256,512]{1,0:T(8,128)(2,1)}, u32[]{:S(2)}) copy-start(bf16[256,512]{1,0:T(8,128)(2,1)} %q_ref.3) | copy-start | bytes 786436
  51.0 15.0 %all-to-all-start.3 = ((bf16[16,16,128]{2,1,0:T(8,128)(2,1)}), bf16[16,16,128]{2,1,0:T(8,128)(2,1)S(1)}, u32[]{:S(2)}, u32[]{:S(2)}) async-start(bf16[16,16,128]{2,1,0:T(8,128)(2,1)} %shard_map.127._), calls=%async_computation.3 | async-start | bytes 131072 | tf_op jit(solution)/shard_map/all_to_all | solution.py:57

commit v8 on v7

--- a/solution.py
+++ b/solution.py
@@ -21,7 +21,7 @@
 bf16 = jnp.bfloat16
 vmem_limit = 32 * 1024 * 1024
 shadow_flops = 5 * 10**9
-first_chip, first_shard = 18, 4
+first_chip, first_shard = 18, 12
 CH = 256
 at_requests, at_lengths, at_offset, at_core = 16, 32, 32 + REQ, 33 + REQ
 at_values, at_info, at_weight, at_end = CH, 2 * CH, 2 * CH + 16, 2 * CH + 16 + 512

time: 67 us -> 66.8 us (level)
  no operation moved by 1% of the time
where the time goes in v8:
time: 66.8 us; the launch traced here: 66.4 us
  starting transfers between devices  30.6 us (46%)
  blocking collectives  25.9 us (39%)
  Pallas kernels  6.05 us (9%)
  waiting for transfers between devices  1.55 us (2%)
  between operations  1.42 us (2%)
  local copies, waits for them, and re-layouts  0.83 us (1%)
    all_to_all x2, blocking collectives, exchange(): lax.all_to_all(blocks, axes, split_axis=0, concat_axis=0, axis_index_grou...  25.9 us
    all_to_all x2, starting transfers between devices, exchange(): lax.all_to_all(blocks, axes, split_axis=0, concat_axis=0, axis_index_grou...  24.5 us
    ppermute x1, starting transfers between devices, on_device(): other = lax.ppermute(own, 'c', [(0, 1), (1, 0)])  6.12 us
    pallas_call x8, Pallas kernels, call(): pl.pallas_call(kernel, out_shape=outs, in_specs=[pl.BlockSpec(memory_spac...  6.05 us
  transfers between devices with their start and end apart: 3, of which 2 were waited for; matrix products, arithmetic and copies ran while one was open for 0% of the time, Pallas kernels for 4%

profile of v8, /device:TPU:1, one launch (start us, length us, event | category | flops | bytes accessed | tf_op | source)
XLA Modules:
  0.0 66.4 jit_solution(6474014652600644997)
XLA Ops:
  0.6 0.0 copy-start.4
  0.6 0.7 %copy-done.4 = bf16[4,512]{1,0:T(4,128)(2,1)S(1)} copy-done((bf16[4,512]{1,0:T(4,128)(2,1)S(1)}, bf16[4,512]{1,0:T(4,128)(2,1)}, u32[]{:S(2)}) %copy-start.4) | copy-done | bytes 4120
  1.3 0.0 copy-start.7
  1.3 0.0 copy-start.8
  1.3 0.0 copy-start.9
  1.3 0.7 %shard_map.122 = (bf16[32,4,512]{2,1,0:T(4,128)(2,1)}, bf16[16,128]{1,0:T(8,128)(2,1)S(1)}) custom-call(bf16[4,512]{1,0:T(4,128)(2,1)S(1)} %copy-done.4), custom_call_target="tpu_custom_call" | custom-call | bytes 139264 | tf_op jit(solution)/shard_map/pallas_call | solution.py:69
  2.0 0.0 copy-start.1
  2.0 0.0 copy-start.2
  2.0 0.0 copy-start.3
  2.0 0.0 copy-start.5
  2.0 12.6 %all-to-all-start = ((bf16[32,4,512]{2,1,0:T(4,128)(2,1)}), bf16[32,4,512]{2,1,0:T(4,128)(2,1)S(1)}, u32[]{:S(2)}, u32[]{:S(2)}) async-start(bf16[32,4,512]{2,1,0:T(4,128)(2,1)} %get-tuple-element.12._), calls=%async_computation | async-start | bytes 262144 | tf_op jit(solution)/shard_map/all_to_all | solution.py:57
  15.2 0.0 copy-done.7
  15.2 0.0 copy-done.8
  15.3 0.0 copy-done.9
  15.3 0.1 add_bitcast_fusion.ints_ref
  15.3 0.0 copy-done.1
  15.4 0.0 copy-done.2
  15.4 0.0 copy-done.3
  15.4 0.2 shard_map.123.own_ref.pack_ref
  15.5 6.1 %collective-permute-start = (bf16[1040,128]{1,0:T(8,128)(2,1)S(1)}, bf16[1040,128]{1,0:T(8,128)(2,1)S(1)}, u32[]{:S(2)}, u32[]{:S(2)}) collective-permute-start(bf16[1040,128]{1,0:T(8,128)(2,1)S(1)} %shard_map.123.own_ref.pack_ref), channel_id=1, source_target_pairs={{0,8},{8,0},{1,9},{9,1},{2,10},{10,2},{3,11},{11,3},{4,12},{12,4},... | collective-permute-start | bytes 798728 | tf_op jit(solution)/shard_map/ppermute | solution.py:308
  21.7 0.0 copy-done.5
  21.7 0.4 shard_map.124
  22.1 0.0 all-to-all-done
  22.2 0.6 collective-permute-done.other_ref
  22.8 1.0 %shard_map.125 = bf16[32,4,640]{2,1,0:T(4,128)(2,1)S(1)} custom-call(bf16[128,512]{1,0:T(8,128)(2,1)S(1)} %reshape.21.q_ref, bf16[1040,128]{1,0:T(8,128)(2,1)S(1)} %shard_map.123.own_ref.pack_ref, bf16[1040,128]{1,0:T(8,128)(2,1)S(1)} %collective-permute-done.other_ref), custom_call_target="tpu_custom_call" | custom-call | bytes 827392 | tf_op jit(solution)/shard_map/pallas_call | solution.py:69
  23.8 0.0 copy-start
  23.9 13.8 %all_to_all.20 = bf16[32,4,640]{2,1,0:T(4,128)(2,1)S(1)} all-to-all(bf16[32,4,640]{2,1,0:T(4,128)(2,1)S(1)} %shard_map.125), channel_id=1, replica_groups={{288,304,320,336,352,368,384,400,416,432,448,464,480,496,0,16,32,48,64,..., dimensions={0} | all-to-all | bytes 327680 | tf_op jit(solution)/shard_map/all_to_all | solution.py:57
  37.7 0.0 copy-done
  37.7 0.3 shard_map.126
  38.0 12.1 %all_to_all.21 = bf16[32,4,512]{2,1,0:T(4,128)(2,1)S(1)} all-to-all(bf16[32,4,512]{2,1,0:T(4,128)(2,1)S(1)} %shard_map.126), channel_id=1, replica_groups={{288,304,320,336,352,368,384,400,416,432,448,464,480,496,0,16,32,48,64,..., dimensions={0} | all-to-all | bytes 262144 | tf_op jit(solution)/shard_map/all_to_all | solution.py:57
  50.2 0.0 copy-start.6
  50.2 0.9 %shard_map.127._ = bf16[16,16,128]{2,1,0:T(8,128)(2,1)} custom-call(bf16[128,512]{1,0:T(8,128)(2,1)S(1)} %reshape.23.rows_ref, bf16[1040,128]{1,0:T(8,128)(2,1)S(1)} %shard_map.123.own_ref.pack_ref, bf16[1040,128]{1,0:T(8,128)(2,1)S(1)} %collective-permute-done.other_ref), custom_call_target="tpu_custom_call" | custom-call | bytes 729088 | tf_op jit(solution)/shard_map/pallas_call | solution.py:69
  51.0 11.9 %all-to-all-start.3 = ((bf16[16,16,128]{2,1,0:T(8,128)(2,1)}), bf16[16,16,128]{2,1,0:T(8,128)(2,1)S(1)}, u32[]{:S(2)}, u32[]{:S(2)}) async-start(bf16[16,16,128]{2,1,0:T(8,128)(2,1)} %shard_map.127._), calls=%async_computation.3 | async-start | bytes 131072 | tf_op jit(solution)/shard_map/all_to_all | solution.py:57
  63.0 0.0 copy-done.6
  63.0 1.9 %shard_map.128 = bf16[256,512]{1,0:T(8,128)(2,1)} custom-call(s32[1,128]{1,0:T(1,128)S(1)} %add_bitcast_fusion.ints_ref, bf16[256,512]{1,0:T(8,128)(2,1)S(1)} %copy-done.6, bf16[1040,128]{1,0:T(8,128)(2,1)S(1)} %shard_map.123.own_ref.pack_ref, bf16[16,16,128]{2,1,0:T(8,128)(2,1)} %shard_map.127._), custom_call_target="tpu_custom_call" | custom-call | flops 5000000000 | bytes 856576 | tf_op jit(solution)/shard_map/pallas_call | solution.py:69
  64.9 0.9 %all-to-all-done.3.terms_ref = bf16[16,16,128]{2,1,0:T(8,128)(2,1)S(1)} async-done(((bf16[16,16,128]{2,1,0:T(8,128)(2,1)}), bf16[16,16,128]{2,1,0:T(8,128)(2,1)S(1)}, u32[]{:S(2)}, u32[]{:S(2)}) %all-to-all-start.3) | async-done | bytes 65568 | tf_op jit(solution)/shard_map/all_to_all | solution.py:57
  65.8 0.6 shard_map.129
  (3 shorter events, 0.1 us)
Async XLA Ops:
  0.6 0.7 %copy-start.4 = (bf16[4,512]{1,0:T(4,128)(2,1)S(1)}, bf16[4,512]{1,0:T(4,128)(2,1)}, u32[]{:S(2)}) copy-start(bf16[4,512]{1,0:T(4,128)(2,1)} %q_ref.2) | copy-start | bytes 12292
  1.3 13.9 %copy-start.7 = (s32[4]{0:T(128)S(1)}, s32[4]{0:T(128)}, u32[]{:S(2)}) copy-start(s32[4]{0:T(128)} %param.20) | copy-start | bytes 52
  1.3 13.9 %copy-start.8 = (s32[16]{0:T(128)S(1)}, s32[16]{0:T(128)}, u32[]{:S(2)}) copy-start(s32[16]{0:T(128)} %param.16) | copy-start | bytes 196
  1.3 13.9 %copy-start.9 = (s32[16,1]{0,1:T(1,128)S(1)}, s32[16,1]{0,1:T(1,128)}, u32[]{:S(2)}) copy-start(s32[16,1]{0,1:T(1,128)} %param.15) | copy-start | bytes 196
  2.0 13.4 %copy-start.1 = (bf16[512,128]{1,0:T(8,128)(2,1)S(1)}, bf16[512,128]{1,0:T(8,128)(2,1)}, u32[]{:S(2)}) copy-start(bf16[512,128]{1,0:T(8,128)(2,1)} %weight_ref.1) | copy-start | bytes 393220
  2.0 13.4 %copy-start.2 = (bf16[256,128]{1,0:T(8,128)(2,1)S(1)}, bf16[256,128]{1,0:T(8,128)(2,1)}, u32[]{:S(2)}) copy-start(bf16[256,128]{1,0:T(8,128)(2,1)} %k_ref.2) | copy-start | bytes 196612
  2.0 13.4 %copy-start.3 = (bf16[256,128]{1,0:T(8,128)(2,1)S(1)}, bf16[256,128]{1,0:T(8,128)(2,1)}, u32[]{:S(2)}) copy-start(bf16[256,128]{1,0:T(8,128)(2,1)} %v_ref.2) | copy-start | bytes 196612
  2.0 19.7 %copy-start.5 = (bf16[4,512,128]{2,1,0:T(8,128)(2,1)S(1)}, bf16[4,512,128]{2,1,0:T(8,128)(2,1)}, u32[]{:S(2)}) copy-start(bf16[4,512,128]{2,1,0:T(8,128)(2,1)} %k_ref.3) | copy-start | bytes 1572868
  2.0 20.1 %all-to-all-start = ((bf16[32,4,512]{2,1,0:T(4,128)(2,1)}), bf16[32,4,512]{2,1,0:T(4,128)(2,1)S(1)}, u32[]{:S(2)}, u32[]{:S(2)}) async-start(bf16[32,4,512]{2,1,0:T(4,128)(2,1)} %get-tuple-element.12._), calls=%async_computation | async-start | bytes 262144 | tf_op jit(solution)/shard_map/all_to_all | solution.py:57
  15.5 7.3 %collective-permute-start = (bf16[1040,128]{1,0:T(8,128)(2,1)S(1)}, bf16[1040,128]{1,0:T(8,128)(2,1)S(1)}, u32[]{:S(2)}, u32[]{:S(2)}) collective-permute-start(bf16[1040,128]{1,0:T(8,128)(2,1)S(1)} %shard_map.123.own_ref.pack_ref), channel_id=1, source_target_pairs={{0,8},{8,0},{1,9},{9,1},{2,10},{10,2},{3,11},{11,3},{4,12},{12,4},... | collective-permute-start | bytes 798728 | tf_op jit(solution)/shard_map/ppermute | solution.py:308
  23.8 13.8 %copy-start = (bf16[4,512,128]{2,1,0:T(8,128)(2,1)S(1)}, bf16[4,512,128]{2,1,0:T(8,128)(2,1)}, u32[]{:S(2)}) copy-start(bf16[4,512,128]{2,1,0:T(8,128)(2,1)} %v_ref.3) | copy-start | bytes 1572868
  50.2 12.8 %copy-start.6 = (bf16[256,512]{1,0:T(8,128)(2,1)S(1)}, bf16[256,512]{1,0:T(8,128)(2,1)}, u32[]{:S(2)}) copy-start(bf16[256,512]{1,0:T(8,128)(2,1)} %q_ref.3) | copy-start | bytes 786436
  51.0 14.7 %all-to-all-start.3 = ((bf16[16,16,128]{2,1,0:T(8,128)(2,1)}), bf16[16,16,128]{2,1,0:T(8,128)(2,1)S(1)}, u32[]{:S(2)}, u32[]{:S(2)}) async-start(bf16[16,16,128]{2,1,0:T(8,128)(2,1)} %shard_map.127._), calls=%async_computation.3 | async-start | bytes 131072 | tf_op jit(solution)/shard_map/all_to_all | solution.py:57
